TPU v7x, 512 devices: a whole 4x4x16 slice. The times are simulated.
512 devices in a mesh: lat: 8 (over z_hi, y), lon: 64 (over z_lo, x, core).
Axes of the slice: x: 4, y: 4, z: 16 (z_hi: 2, z_lo: 8; z = z_hi * 8 + z_lo), core: 2. Of those that a mesh axis runs over, the one named last changes fastest.
Arguments:
- tokens: bfloat16 [1, 4, 96, 384, 192], P(None, None, 'lat', 'lon'), may hold values from -6 to 6
- fine_gain: float32 [192], replicated, may hold values from 0.25 to 1.75
- fine_shift: float32 [192], replicated, may hold values from -3 to 3
- fine_qkv: bfloat16 [192, 576], replicated, may hold values from -0.4375 to 0.4375
- fine_qkv_bias: float32 [576], replicated, may hold values from -8 to 8
- fine_proj: bfloat16 [192, 192], replicated, may hold values from -0.4375 to 0.4375
- fine_proj_bias: float32 [192], replicated, may hold values from -3 to 3
- fine_table: bfloat16 [16, 39744], P('lat'), may hold values from -5 to 305
- merge_gain: float32 [768], replicated, may hold values from 0.25 to 1.75
- merge_shift: float32 [768], replicated, may hold values from -3 to 3
- merge_weight: bfloat16 [768, 384], replicated, may hold values from -0.21875 to 0.21875
- coarse_gain: float32 [384], replicated, may hold values from 0.25 to 1.75
- coarse_shift: float32 [384], replicated, may hold values from -3 to 3
- coarse_qkv: bfloat16 [384, 1152], replicated, may hold values from -0.3125 to 0.3125
- coarse_qkv_bias: float32 [1152], replicated, may hold values from -8 to 8
- coarse_proj: bfloat16 [384, 384], replicated, may hold values from -0.3125 to 0.3125
- coarse_proj_bias: float32 [384], replicated, may hold values from -3 to 3
- coarse_table: bfloat16 [16, 39744], P('lat'), may hold values from -5 to 305
- cotangent: bfloat16 [1, 4, 48, 192, 384], P(None, None, 'lat', 'lon'), may hold values from -6 to 6
Outputs:
- coarse_out: bfloat16 [1, 4, 48, 192, 384], P(None, None, 'lat', 'lon')
- token_grad: bfloat16 [1, 4, 96, 384, 192], P(None, None, 'lat', 'lon')
- param_grads: float32 [1037184], P('lon')
- fine_table_grad: float32 [16, 39744], P('lat')
- coarse_table_grad: float32 [16, 39744], P('lat')
All inputs are finite; a program needn't handle non-finite values.
Results may differ from a plain program's by a relative error of at most 0.035.
Values may be sent and summed in bfloat16 or wider, within the bound.
A program may use at most 128 MiB of HBM per device.

v0:
```python
import functools
import math

import jax
import jax.numpy as jnp
from jax import lax
from jax.experimental import pallas as pl
from jax.experimental.pallas import tpu as pltpu
from jax.sharding import PartitionSpec as P

HEAD = 32
HEADS_F = 6
HEADS_C = 12
C_F = 192
C_C = 384
SPAN = 23
EPS = 1e-05
NEGATIVE = -1e30
MESH = pl.DeviceIdType.MESH
F32 = jnp.float32
BF16 = jnp.bfloat16
MIB = 1024 * 1024
VMEM_BYTES = 60 * MIB

LOW, MID, TOP = (0, 80, 224)
PARAMS = 1037184
TABLE_ROWS = 2048
FINE = 304
SIDE = 80
COARSE = 80
PART_C, PART_A, PART_B, PART_Q, PART_END = (0, 256, 688, 928, 1792)


def whole(x, n):
    return jnp.floor((x + 0.5) * (1.0 / n))


def rest(x, n):
    return x - n * whole(x, n)


def down_rows(n):
    return lax.broadcasted_iota(jnp.int32, (n, 1), 0).astype(F32)


def along_lanes(n):
    return lax.broadcasted_iota(jnp.int32, (1, n), 1).astype(F32)


def match(a, b):
    return jnp.where(a == b, 1.0, 0.0).astype(BF16)


def fine_row(zone, zq, row, col):
    low = LOW + zone * 40 + (zq * 3 + row) * 6 + col
    mid = MID + zone * 72 + (zq * 6 + row - 3) * 6 + col
    top = TOP + zone * 40 + (zq * 3 + row - 9) * 6 + col
    return jnp.where(row < 3, low, jnp.where(row < 9, mid, top))


def fine_order():
    at = down_rows(FINE)
    low, top = (at < MID, at >= TOP)
    edge = jnp.where(top, at - TOP, at)
    mid = at - MID
    in_edge = low | top
    part = rest(edge, 40)
    zone = jnp.where(in_edge, whole(edge, 40), whole(mid, 72))
    zq = jnp.where(in_edge, whole(part, 18), whole(rest(mid, 72), 36))
    row = jnp.where(
        in_edge,
        whole(rest(part, 18), 6) + jnp.where(top, 9.0, 0.0),
        3 + whole(rest(mid, 36), 6),
    )
    col = jnp.where(in_edge, rest(part, 6), rest(mid, 6))
    code = (row * 6 + col) * 4 + rest(2 * zone + zq + 1, 4)
    return match(jnp.where(in_edge & (part >= 36), -1.0, code), along_lanes(288))


def coarse_place(at):
    part = rest(at, 40)
    return (whole(at, 40), whole(part, 18), whole(rest(part, 18), 3), rest(part, 3), part < 36)


def coarse_order():
    zone, zq, row, col, valid = coarse_place(down_rows(COARSE))
    code = (row * 3 + col) * 4 + 2 * zone + zq
    return match(jnp.where(valid, code, -1.0), along_lanes(72))


def quartet_order():
    at = down_rows(4 * COARSE)
    p = whole(at, COARSE)
    zone, zq, row, col, valid = coarse_place(rest(at, COARSE))
    rolled = rest(2 * zone + zq + 3, 4)
    source = fine_row(
        whole(rolled, 2), rest(rolled, 2), 2 * row + rest(p, 2), 2 * col + whole(p, 2)
    )
    return match(jnp.where(valid, source, -1.0), along_lanes(FINE))


def head_rows(heads, lats, cols, tokens, block):
    at = down_rows(block * cols)
    part = rest(at, block)
    h = whole(part, 2 * lats)
    zq = whole(rest(part, 2 * lats), lats)
    code = (zq * lats + rest(part, lats)) * cols + whole(at, block)
    valid = part < heads * 2 * lats
    head = jnp.where(valid, h, -1.0)
    mask = match(head, whole(along_lanes(heads * HEAD), HEAD)).astype(F32)
    return (match(jnp.where(valid, code, -1.0), along_lanes(tokens)), mask, zq)


def pair_keys(size, half):
    u = along_lanes(size)
    if size == 144:
        source, part = (whole(u, 72), rest(u, 72))
        zk, ak, valid = (whole(part, 36), whole(rest(part, 36), 6), part >= 0)
    else:
        slot, part = (whole(u, 40), rest(u, 40))
        source = rest(slot, 2)
        zk = whole(part, 18)
        ak = 3 * whole(slot, 2) + whole(rest(part, 18), 6)
        valid = part < 36
    return (zk, ak, rest(part, 6) + 6 * jnp.abs(half - source), valid)


def group_keys():
    u = along_lanes(160)
    part = rest(u, 40)
    zk, ak = (whole(part, 18), whole(rest(part, 18), 3))
    return (zk, ak, rest(part, 3) + 3 * whole(u, 40), part < 36)


def toeplitz(keys, cols, shift):
    zk, ak, col, valid = keys
    at = down_rows(384)
    tail = at >= 256
    level = jnp.where(tail, whole(at - 256, 64), whole(at, 128))
    entry = jnp.where(tail, 128 + rest(at, 64), rest(at, 128))
    code = (level * 6 + whole(entry, SPAN)) * 64 + rest(entry, SPAN)
    code = jnp.where(entry < 138, code, -1.0)
    key_code = jnp.where(valid, (zk * 6 + ak) * 64 - col + shift + 11, -100.0)
    return [match(code, key_code + oq) for oq in range(cols)]


def table_lanes(zk):
    entry = down_rows(138)
    return match(
        jnp.where(entry < 128, zk * 128 + entry, 256 + zk * 64 + entry - 128), along_lanes(384)
    )


def table_rows(kind, zk):
    if kind == "q":
        at = down_rows(288)
        part = rest(at, 144)
        aq = rest(part, 6)
        lead = (whole(aq, 3) * 2 + whole(at, 144)) * HEADS_C + whole(part, 12)
        zq = whole(rest(part, 12), 6)
        return match(((lead * 2 + zq) * 2 + zk) * 3 + rest(aq, 3), along_lanes(576))
    if kind == "a":
        at, block, lats, first = (down_rows(144), 72, 6, 0)
    else:
        at, block, lats, first = (down_rows(80), 40, 3, 3 if kind == "c" else 0)
    part = rest(at, block)
    lead = whole(at, block) * HEADS_F + whole(part, 2 * lats)
    zq = whole(rest(part, 2 * lats), lats)
    code = ((lead * 2 + zq) * 2 + zk) * 6 + rest(part, lats) + first
    return match(jnp.where(part < 12 * lats, code, -1.0), along_lanes(288))


def dot(a, b):
    return jnp.dot(a.astype(BF16), b.astype(BF16), preferred_element_type=F32)


def dot_nt(a, b):
    return lax.dot_general(
        a.astype(BF16), b.astype(BF16), (((1,), (1,)), ((), ())), preferred_element_type=F32
    )


def dot_tn(a, b):
    return lax.dot_general(
        a.astype(BF16), b.astype(BF16), (((0,), (0,)), ((), ())), preferred_element_type=F32
    )


def rounded(value):
    return value.astype(BF16).astype(F32)


def norm_parts(volume):
    centre = volume - jnp.mean(volume, -1, keepdims=True)
    spread = jnp.mean(centre * centre, -1, keepdims=True)
    scale = lax.rsqrt(spread + EPS)
    return (centre * scale, scale)


def norm_back(hat, scale, grad, gain):
    inner = grad * gain
    return scale * (
        inner
        - jnp.mean(inner, -1, keepdims=True)
        - hat * jnp.mean(inner * hat, -1, keepdims=True)
    )


def column_sum(value):
    return jnp.sum(value, 0, keepdims=True)


def attend(queries, keys, values, rows, mask, bias):
    packed = dot(rows, queries) * mask
    scores = dot_nt(packed, keys) * HEAD ** (-0.5) + bias
    weights = jnp.exp(scores - jnp.max(scores, -1, keepdims=True))
    probs = weights / jnp.sum(weights, -1, keepdims=True)
    mixture = dot(probs, values) * mask
    return (probs, dot_tn(rows, mixture))


def attend_back(queries, keys, values, rows, mask, probs, mixture_grad, toep, block):
    factor = HEAD ** (-0.5)
    packed = dot(rows, queries) * mask
    grad = dot(rows, mixture_grad) * mask
    value_grad = dot_tn(probs, grad)
    prob_grad = dot_nt(grad, values)
    score_grad = probs * (prob_grad - jnp.sum(prob_grad * probs, -1, keepdims=True))
    query_grad = dot_tn(rows, dot(score_grad, keys) * factor * mask)
    key_grad = dot_tn(score_grad, packed) * factor
    table = None
    for oq, select in enumerate(toep):
        part = dot_nt(score_grad[oq * block : (oq + 1) * block], select)
        table = part if table is None else table + part
    return (query_grad, key_grad, value_grad, table)


def lasting(micros):
    return pl.CostEstimate(flops=0, bytes_accessed=int(micros * 3.69e6), transcendentals=0)


def call(body, outs, args, scratch, name, micros, in_place=(), limit=VMEM_BYTES):
    vmem = pl.BlockSpec(memory_space=pltpu.VMEM)
    away = pl.BlockSpec(memory_space=pltpu.HBM)
    return pl.pallas_call(
        body,
        out_shape=tuple(jax.ShapeDtypeStruct(shape, dtype) for shape, dtype in outs),
        in_specs=[away if at in in_place else vmem for at in range(len(args))],
        out_specs=(vmem,) * len(outs),
        scratch_shapes=list(scratch),
        compiler_params=pltpu.CompilerParams(vmem_limit_bytes=limit),
        cost_estimate=lasting(micros),
        name=name,
    )(*args)


def vector(ref):
    return ref[...].reshape(1, -1)


def query_half():
    return 1 - lax.rem(lax.axis_index("lon"), 2)


def packed_side(value):
    tail = jnp.concatenate([value[0:40, 128:192], value[40:80, 128:192]], 1)
    return jnp.concatenate([value[:, 0:128], tail, jnp.zeros((8, 128), value.dtype)], 0)


def unpacked_side(block):
    tail = jnp.concatenate([block[80:120, 0:64], block[80:120, 64:128]], 0)
    return jnp.concatenate([block[0:80, :], tail], 1)


def lane_blocks(pieces):
    blocks = []
    for a, b in zip(pieces[::2], pieces[1::2]):
        blocks += [a[:, 0:128], jnp.concatenate([a[:, 128:192], b[:, 0:64]], 1), b[:, 64:192]]
    return blocks


def partner_of(lon, count):
    odd = lax.rem(lon, 2)
    return lax.rem(lon + 2 * odd - 1 + count, count)


def ring_positions():
    lat_count, lon_count = (lax.axis_size("lat"), lax.axis_size("lon"))
    lat, lon = (lax.axis_index("lat"), lax.axis_index("lon"))
    up = lax.rem(lat + 1, lat_count)
    down = lax.rem(lat + lat_count - 1, lat_count)
    return (lat, lon, up, down, partner_of(lon, lon_count))


def meet(peers):
    barrier = pltpu.get_barrier_semaphore()
    for peer in peers:
        pl.semaphore_signal(barrier, inc=1, device_id=peer, device_id_type=MESH)
    pl.semaphore_wait(barrier, len(peers))


def start_copy(src, dst, send_sem, recv_sem, peer):
    copy = pltpu.make_async_remote_copy(
        src_ref=src,
        dst_ref=dst,
        send_sem=send_sem,
        recv_sem=recv_sem,
        device_id=peer,
        device_id_type=MESH,
    )
    copy.start()
    return copy


def exchange(sends, send_sems, recv_sems):
    copies = []
    for at, (src, dst, peer) in enumerate(sends):
        copies.append(start_copy(src, dst, send_sems.at[at], recv_sems.at[at], peer))
    for copy in copies:
        copy.wait_recv()
    for copy in copies:
        copy.wait_send()


def exchange_call(body, outs, args, scratch, counts, collective_id, name, micros):
    vmem = pl.BlockSpec(memory_space=pltpu.VMEM)
    sem = pltpu.SemaphoreType.DMA
    return pl.pallas_call(
        body,
        out_shape=tuple(jax.ShapeDtypeStruct(shape, dtype) for shape, dtype in outs),
        in_specs=[vmem] * len(args),
        out_specs=(vmem,) * len(outs),
        scratch_shapes=list(scratch) + [sem((count,)) for count in counts for _ in range(2)],
        compiler_params=pltpu.CompilerParams(
            collective_id=collective_id, has_side_effects=True, vmem_limit_bytes=VMEM_BYTES
        ),
        cost_estimate=lasting(micros),
        name=name,
    )(*args)


def halo_body(x_ref, low_ref, high_ref, tab_ref, *refs):
    outs, bufs, (ss, rs, ts, tr) = (refs[:6], refs[6:12], refs[12:])
    par, upo, upp, dno, dnp, tab = bufs
    lat, lon, up, down, partner = ring_positions()
    size = tab.shape[0]
    rank = lax.rem(lon, size)
    others = [lax.rem(rank + d, size) for d in range(1, size)]
    near = [(lat, lon - rank + other) for other in others]
    beside = (lat, partner)
    meet([beside, (up, lon), (down, lon)] + near)
    x_copy = start_copy(x_ref, par, ss.at[0], rs.at[0], beside)
    low_copy = start_copy(low_ref, upo, ss.at[1], rs.at[1], (down, lon))
    high_copy = start_copy(high_ref, dno, ss.at[2], rs.at[2], (up, lon))
    table_copy = start_copy(tab_ref.at[rank], tab.at[rank], ss.at[3], rs.at[3], (up, lon))
    copies = [x_copy, low_copy, high_copy, table_copy]
    low_copy.wait_recv()
    relays = [start_copy(upo, upp, ss.at[4], rs.at[4], beside)]
    high_copy.wait_recv()
    relays.append(start_copy(dno, dnp, ss.at[5], rs.at[5], beside))
    table_copy.wait_recv()
    for d, peer in enumerate(near):
        relays.append(start_copy(tab.at[rank], tab.at[rank], ts.at[d], tr.at[d], peer))
    x_copy.wait_recv()
    for copy in relays:
        copy.wait_recv()
    for copy in copies + relays:
        copy.wait_send()
    for out, buf in zip(outs, bufs):
        out[...] = buf[...]


def group_body(own_ref, out_ref, buf, ss, rs):
    lat, lon = (lax.axis_index("lat"), lax.axis_index("lon"))
    place = lax.rem(lon, 4)
    others = [lax.rem(place + d, 4) for d in range(1, 4)]
    peers = [(lat, lon - place + other) for other in others]
    meet(peers)
    buf[place] = own_ref[...]
    exchange([(own_ref, buf.at[place], peer) for peer in peers], ss, rs)
    out_ref[...] = buf[...]


def ungroup_body(parts_ref, out_ref, buf, ss, rs):
    lat, lon = (lax.axis_index("lat"), lax.axis_index("lon"))
    place = lax.rem(lon, 4)
    others = [lax.rem(place + d, 4) for d in range(1, 4)]
    peers = [(lat, lon - place + other) for other in others]
    meet(peers)
    exchange(
        [(parts_ref.at[other], buf.at[d], peers[d]) for d, other in enumerate(others)], ss, rs
    )
    total = parts_ref[place].astype(F32)
    for d in range(3):
        total = total + buf[d].astype(F32)
    out_ref[...] = total


def spread(kind, table):
    total = None
    for zk in range(2):
        part = dot(dot(table_rows(kind, zk), table), table_lanes(zk))
        total = part if total is None else total + part
    return total


def bias_rows(table, toep, zone, block):
    rows = table[zone * block : (zone + 1) * block]
    return jnp.concatenate([dot(rows, select) for select in toep], 0)


def banned(keys, zq, zone):
    ban = jnp.where(keys[3], 0.0, NEGATIVE)
    if zone == 1:
        ban = ban + jnp.where(zq == keys[0], 0.0, NEGATIVE)
    return ban


def fetch_groups(stage, ref):
    rows, cols = ref.shape[:2]
    for row in range(rows):
        for col in range(cols):
            at = (row * cols + col) * 4
            stage[at : at + 4, :] = ref[row, col].astype(F32)


def store_groups(ref, stage):
    rows, cols = ref.shape[:2]
    for row in range(rows):
        for col in range(cols):
            at = (row * cols + col) * 4
            ref[row, col] = stage[at : at + 4, :].astype(BF16)


def prepare_body(x_ref, tf_ref, own_out, low_out, high_out, tab_out, stage):
    fetch_groups(stage, x_ref)
    tokens = dot(fine_order(), stage[...])
    own_out[...] = tokens.astype(BF16)
    low_out[...] = packed_side(tokens[LOW : LOW + SIDE]).astype(BF16)
    high_out[...] = packed_side(tokens[TOP : TOP + SIDE]).astype(BF16)
    table = spread("c", tf_ref[288:576, :])
    pieces = [table[:, c * 128 : (c + 1) * 128] for c in range(3)]
    block = jnp.concatenate(pieces + [jnp.zeros((16, 128), F32)], 0).astype(BF16)
    size = tab_out.shape[1]
    for place in range(tab_out.shape[0]):
        tab_out[place] = block[place * size : (place + 1) * size, :]


def fine_kinds():
    half = query_half().astype(F32)
    rows_a, mask_a, zq_a = head_rows(HEADS_F, 6, 6, 72, 72)
    rows_b, mask_b, zq_b = head_rows(HEADS_F, 3, 6, 40, 40)
    keys_a, keys_b = (pair_keys(144, half), pair_keys(160, half))
    toep_a, toep_b = (toeplitz(keys_a, 6, 6 * half), toeplitz(keys_b, 6, 6 * half))
    mid = (rows_a, mask_a, zq_a, keys_a, toep_a, 72)
    edge = (rows_b, mask_b, zq_b, keys_b, toep_b, 40)
    return {"a": mid, "b": edge, "c": edge}


def fine_windows(zone):
    edge = zone * 40
    return (
        ("a", (MID + zone * 72, 72), [(0, MID + zone * 72, 72), (1, MID + zone * 72, 72)]),
        ("b", (TOP + edge, 40), [(0, TOP + edge, 40), (1, TOP + edge, 40), (2, edge, 40), (3, edge, 40)]),
        ("c", (LOW + edge, 40), [(4, edge, 40), (5, edge, 40), (0, LOW + edge, 40), (1, LOW + edge, 40)]),
    )


SOURCES = (0, FINE, 2 * FINE, 2 * FINE + SIDE, 2 * FINE + 2 * SIDE, 2 * FINE + 3 * SIDE)
ALL_ROWS = 2 * FINE + 4 * SIDE


def gathered(ref, pieces):
    return jnp.concatenate(
        [ref[SOURCES[source] + start : SOURCES[source] + start + count, :] for source, start, count in pieces],
        0,
    )


def fine_forward_body(
    own_ref,
    par_ref,
    upo_ref,
    upp_ref,
    dno_ref,
    dnp_ref,
    gain_ref,
    shift_ref,
    qkv_ref,
    qkv_bias_ref,
    proj_ref,
    proj_bias_ref,
    merge_gain_ref,
    merge_shift_ref,
    merge_ref,
    coarse_gain_ref,
    coarse_shift_ref,
    tf_ref,
    tp_ref,
    hat_out,
    normed,
    q_out,
    k_out,
    v_out,
    probs_a,
    probs_b,
    probs_c,
    mix_out,
    fine_out,
    merged_out,
    coarse_out,
    cnorm_out,
):
    gain, shift = (vector(gain_ref), vector(shift_ref))
    own = own_ref[...].astype(F32)
    for place, tokens in enumerate(
        [own, par_ref[...].astype(F32)]
        + [unpacked_side(ref[...].astype(F32)) for ref in (upo_ref, upp_ref, dno_ref, dnp_ref)]
    ):
        hat, _ = norm_parts(tokens)
        at = slice(SOURCES[place], SOURCES[place] + tokens.shape[0])
        hat_out[at, :] = hat
        normed[at, :] = (hat * gain + shift).astype(BF16)
    bias = vector(qkv_bias_ref)
    q_out[...] = rounded(dot(normed[0:FINE, :], qkv_ref[:, 0:C_F]) + bias[:, 0:C_F])
    k_out[...] = rounded(dot(normed[...], qkv_ref[:, C_F : 2 * C_F]) + bias[:, C_F : 2 * C_F])
    v_out[...] = rounded(dot(normed[...], qkv_ref[:, 2 * C_F :]) + bias[:, 2 * C_F :])
    tables = {
        "a": spread("a", tf_ref[0:288, :]),
        "b": spread("b", tf_ref[288:576, :]),
        "c": jnp.concatenate([tp_ref[c * 80 : (c + 1) * 80, :].astype(F32) for c in range(3)], 1),
    }
    lat = lax.axis_index("lat")
    late = along_lanes(160) >= 80
    edges = {
        "a": 0.0,
        "b": jnp.where(late & (lat == lax.axis_size("lat") - 1), NEGATIVE, 0.0),
        "c": jnp.where(jnp.logical_not(late) & (lat == 0), NEGATIVE, 0.0),
    }
    kinds = fine_kinds()
    probs_refs = {"a": probs_a, "b": probs_b, "c": probs_c}
    mixtures = {}
    for zone in range(2):
        for name, (start, count), pieces in fine_windows(zone):
            rows, mask, zq, keys, toep, block = kinds[name]
            probs_ref = probs_refs[name]
            bias = bias_rows(tables[name], toep, zone, block) + banned(keys, zq, zone) + edges[name]
            probs, mixture = attend(
                q_out[start : start + count, :],
                gathered(k_out, pieces),
                gathered(v_out, pieces),
                rows,
                mask,
                bias,
            )
            probs_ref[zone] = probs
            mixtures[name, zone] = mixture
    mixture = jnp.concatenate([mixtures[name, zone] for name in "cab" for zone in range(2)], 0)
    mix_out[...] = mixture.astype(BF16)
    attn = rounded(dot(mixture, proj_ref[...]) + vector(proj_bias_ref))
    fine = rounded(own + attn)
    fine_out[...] = fine.astype(BF16)
    quartet = dot(quartet_order(), fine)
    parts = [quartet[p * COARSE : (p + 1) * COARSE] for p in range(4)]
    hats, _ = quartet_norm(parts)
    coarse = None
    gain, shift = (vector(merge_gain_ref), vector(merge_shift_ref))
    for p in range(4):
        at = slice(p * C_F, (p + 1) * C_F)
        value = (hats[p] * gain[:, at] + shift[:, at]).astype(BF16)
        merged_out[p] = value
        part = dot(value, merge_ref[p * C_F : (p + 1) * C_F, :])
        coarse = part if coarse is None else coarse + part
    coarse = rounded(coarse)
    coarse_out[...] = coarse
    hat, _ = norm_parts(coarse)
    cnorm_out[...] = (hat * vector(coarse_gain_ref) + vector(coarse_shift_ref)).astype(BF16)


def quartet_norm(parts):
    width = 4.0 * C_F
    mean = sum(jnp.sum(part, -1, keepdims=True) for part in parts) / width
    centres = [part - mean for part in parts]
    spread = sum(jnp.sum(c * c, -1, keepdims=True) for c in centres) / width
    scale = lax.rsqrt(spread + EPS)
    return ([c * scale for c in centres], scale)


def coarse_body(
    group_ref,
    own_ref,
    coarse_ref,
    cot_ref,
    qkv_ref,
    qkv_bias_ref,
    proj_ref,
    proj_bias_ref,
    tc_ref,
    out_ref,
    parts_out,
    own_out,
    flat_out,
    table_out,
    cot_out,
    stage,
    keys,
    values,
):
    fetch_groups(stage, cot_ref)
    order = coarse_order()
    cot = dot(order, stage[...])
    cot_out[...] = cot
    bias = vector(qkv_bias_ref)
    wide = [slice(i * C_C, (i + 1) * C_C) for i in range(3)]
    queries = rounded(dot(own_ref[...], qkv_ref[:, wide[0]]) + bias[:, wide[0]])
    group = jnp.concatenate([group_ref[g] for g in range(4)], 0)
    keys[...] = rounded(dot(group, qkv_ref[:, wide[1]]) + bias[:, wide[1]])
    values[...] = rounded(dot(group, qkv_ref[:, wide[2]]) + bias[:, wide[2]])
    mixture_grad = rounded(dot_nt(cot, proj_ref[...]))
    rows, mask, zq = head_rows(HEADS_C, 6, 3, 40, 144)
    cells = group_keys()
    toep = toeplitz(cells, 3, 3 * lax.rem(lax.axis_index("lon"), 4).astype(F32))
    table_in = spread("q", tc_ref[...])
    mixtures, query_grads, grads = ([], [], [])
    for zone in range(2):
        here = slice(zone * 40, (zone + 1) * 40)
        at = [slice(g * COARSE + zone * 40, g * COARSE + zone * 40 + 40) for g in range(4)]
        k = jnp.concatenate([keys[there, :] for there in at], 0)
        v = jnp.concatenate([values[there, :] for there in at], 0)
        bias = bias_rows(table_in, toep, zone, 144) + banned(cells, zq, 0)
        probs, mixture = attend(queries[here], k, v, rows, mask, bias)
        dq, dk, dv, table = attend_back(
            queries[here], k, v, rows, mask, probs, mixture_grad[here], toep, 144
        )
        table_out[zone * 144 : (zone + 1) * 144, :] = table
        mixtures.append(mixture)
        query_grads.append(dq)
        grads.append((dk, dv))
    key_grad, value_grad = (
        rounded(
            jnp.concatenate(
                [grads[zone][i][g * 40 : (g + 1) * 40] for g in range(4) for zone in range(2)], 0
            )
        )
        for i in range(2)
    )
    query_grad = jnp.concatenate(query_grads, 0)
    part = dot_nt(key_grad, qkv_ref[:, wide[1]]) + dot_nt(value_grad, qkv_ref[:, wide[2]])
    for g in range(4):
        parts_out[g] = part[g * COARSE : (g + 1) * COARSE].astype(BF16)
    own_out[...] = dot_nt(query_grad, qkv_ref[:, wide[0]])
    for i, (norm, grad) in enumerate(
        ((own_ref[...], query_grad), (group, key_grad), (group, value_grad))
    ):
        weight = dot_tn(norm, grad)
        sums = column_sum(grad)
        for c in range(3):
            lanes = slice(c * 128, (c + 1) * 128)
            flat_out[pl.ds(3 * i + c, C_C, stride=9), :] = weight[:, lanes]
            flat_out[3456 + 3 * i + c : 3457 + 3 * i + c, :] = sums[:, lanes]
    mixture = jnp.concatenate(mixtures, 0)
    flat_store(flat_out, 3465, dot_tn(mixture, cot))
    flat_store(flat_out, 4617, column_sum(cot))
    attn = rounded(dot(mixture, proj_ref[...]) + vector(proj_bias_ref))
    stage[...] = dot_tn(order, coarse_ref[...] + attn)
    store_groups(out_ref, stage)


def flat_store(flat, start, matrix):
    height, width = matrix.shape
    step = width // 128
    for c in range(step):
        lanes = slice(c * 128, (c + 1) * 128)
        if height == 1:
            flat[start + c : start + c + 1, :] = matrix[:, lanes]
        else:
            flat[pl.ds(start + c, height, stride=step), :] = matrix[:, lanes]


def keep_square(square, matrix):
    height = matrix.shape[0]
    square[0, 0:height, :] = matrix[:, 0:128]
    square[1, 0:height, 0:64] = matrix[:, 128:192]


def every_other(square, start):
    take = pl.ds(start, 96, stride=2)
    return jnp.concatenate([square[0, take, :], square[1, take, :][:, 0:64]], 1)


def block_store(flat, start, blocks):
    for c, block in enumerate(blocks):
        if block.shape[0] == 1:
            flat[start + c : start + c + 1, :] = block
        else:
            flat[pl.ds(start + c, block.shape[0], stride=len(blocks)), :] = block


def fine_back_body(
    starts,
    rows,
    part_ref,
    own_part_ref,
    cot_ref,
    coarse_ref,
    merged_ref,
    fine_ref,
    hat_ref,
    normed_ref,
    mix_ref,
    q_ref,
    k_ref,
    v_ref,
    probs_a,
    probs_b,
    probs_c,
    qkv_ref,
    cgain_ref,
    merge_gain_ref,
    merge_ref,
    proj_ref,
    flat_c,
    table_q,
    fog_out,
    own_out,
    par_out,
    upo_out,
    upp_out,
    dno_out,
    dnp_out,
    pieces_out,
    kgrad,
    vgrad,
    flat,
    tables,
    square,
):
    norm_grad = part_ref[...] + own_part_ref[...]
    hat, scale = norm_parts(coarse_ref[...])
    flat_store(flat, 3477, column_sum(norm_grad * hat))
    flat_store(flat, 3480, column_sum(norm_grad))
    coarse_grad = rounded(cot_ref[...] + norm_back(hat, scale, norm_grad, vector(cgain_ref)))
    quartet_sel = quartet_order()
    quartet = dot(quartet_sel, fine_ref[...])
    hats, scale = quartet_norm([quartet[p * COARSE : (p + 1) * COARSE] for p in range(4)])
    inners, gains, shifts = ([], [], [])
    merge_gain = vector(merge_gain_ref)
    for p in range(4):
        at = slice(p * C_F, (p + 1) * C_F)
        flat_store(flat, 1173 + 3 * p * C_F, dot_tn(merged_ref[p], coarse_grad))
        grad = dot_nt(coarse_grad, merge_ref[at, :])
        gains.append(column_sum(grad * hats[p]))
        shifts.append(column_sum(grad))
        inners.append(grad * merge_gain[:, at])
    block_store(flat, 1161, lane_blocks(gains))
    block_store(flat, 1167, lane_blocks(shifts))
    width = 4.0 * C_F
    first = sum(jnp.sum(inner, -1, keepdims=True) for inner in inners) / width
    second = sum(jnp.sum(i * h, -1, keepdims=True) for i, h in zip(inners, hats)) / width
    grads = jnp.concatenate([scale * (i - first - h * second) for i, h in zip(inners, hats)], 0)
    high = rounded(grads)
    attn_grad = dot_tn(quartet_sel, high)
    fog_out[...] = attn_grad + dot_tn(quartet_sel, grads - high)
    mixture_grad = rounded(dot_nt(attn_grad, proj_ref[...]))
    weight = dot_tn(mix_ref[...], attn_grad)
    corner = weight[0:1]
    keep_square(square, jnp.concatenate([weight, column_sum(attn_grad)], 0))
    block_store(flat, 873, lane_blocks([every_other(square, 1), every_other(square, 2)]))
    kinds = fine_kinds()
    places = {"a": (PART_A, probs_a), "b": (PART_B, probs_b), "c": (PART_C, probs_c)}
    query_grads = {}
    for zone in range(2):
        for name, (start, count), pieces in fine_windows(zone):
            rows_at, mask, _, _, toep, block = kinds[name]
            table_at, probs_ref = places[name]
            dq, dk, dv, table = attend_back(
                q_ref[start : start + count, :],
                gathered(k_ref, pieces),
                gathered(v_ref, pieces),
                rows_at,
                mask,
                probs_ref[zone],
                mixture_grad[start : start + count],
                toep,
                block,
            )
            query_grads[name, zone] = dq
            for c in range(3):
                at = table_at + (2 * c + zone) * block
                tables[at : at + block, :] = table[:, c * 128 : (c + 1) * 128]
            at = 0
            for source, begin, size in pieces:
                to = slice(SOURCES[source] + begin, SOURCES[source] + begin + size)
                kgrad[to, :] = rounded(dk[at : at + size])
                vgrad[to, :] = rounded(dv[at : at + size])
                at += size
    query_grad = jnp.concatenate([query_grads[name, zone] for name in "cab" for zone in range(2)], 0)
    part = dot_nt(kgrad[...], qkv_ref[:, C_F : 2 * C_F]) + dot_nt(vgrad[...], qkv_ref[:, 2 * C_F :])
    own = part[0:FINE] + dot_nt(query_grad, qkv_ref[:, 0:C_F])
    own_out[...] = own
    par_out[...] = part[FINE : 2 * FINE].astype(BF16)
    for place, out in enumerate((upo_out, upp_out, dno_out, dnp_out)):
        at = SOURCES[2 + place]
        out[...] = packed_side(part[at : at + SIDE]).astype(BF16)
    hat_grad = column_sum(own * hat_ref[0:FINE, :])
    hat_grad += column_sum(part[FINE:] * hat_ref[FINE:, :])
    block_store(
        flat, 0, lane_blocks([hat_grad, column_sum(own) + column_sum(part[FINE:])])
    )
    evens, odds, sums = ([], [], [])
    for norm, grad in (
        (normed_ref[0:FINE, :], query_grad),
        (normed_ref[...], kgrad[...]),
        (normed_ref[...], vgrad[...]),
    ):
        keep_square(square, dot_tn(norm, grad))
        evens.append(every_other(square, 0))
        odds.append(every_other(square, 1))
        sums.append(column_sum(grad))
    block_store(flat, 3, lane_blocks(evens + odds))
    block_store(flat, 867, lane_blocks(sums + [corner]))
    tables[240:PART_A, :] = jnp.zeros((PART_A - 240, 128), F32)
    tables[PART_END:, :] = jnp.zeros((TABLE_ROWS - PART_END, 128), F32)
    for c in range(3):
        at = PART_Q + 288 * c
        tables[at : at + 288, :] = table_q[:, c * 128 : (c + 1) * 128]
    split = 3483
    trows = TABLE_ROWS // len(starts)
    for place, start in starts:
        end = start + rows
        if start < split:
            size = min(end, split) - start
            value = flat[start : start + size, :]
            if end > split:
                value = jnp.concatenate([value, flat_c[0 : end - split, :]], 0)
        else:
            size = min(end, 8103) - start
            value = flat_c[start - split : start - split + size, :]
            if size < rows:
                value = jnp.concatenate([value, jnp.zeros((rows - size, 128), F32)], 0)
        pieces_out[place, 0:rows, :] = value.astype(BF16)
        pieces_out[place, rows:, :] = tables[place * trows : (place + 1) * trows, :].astype(BF16)


def final_body(
    x_ref,
    gain_ref,
    fog_ref,
    own_ref,
    par_ref,
    low_ref,
    high_ref,
    t_ref,
    token_out,
    fine_out,
    coarse_out,
    stage,
    grad,
):
    grad[...] = own_ref[...] + par_ref[...].astype(F32)
    grad[LOW : LOW + SIDE, :] += unpacked_side(low_ref[...].astype(F32))
    grad[TOP : TOP + SIDE, :] += unpacked_side(high_ref[...].astype(F32))
    hat, scale = norm_parts(x_ref[...].astype(F32))
    total = fog_ref[...] + norm_back(hat, scale, rounded(grad[...]), vector(gain_ref))
    stage[...] = dot_tn(fine_order(), total)
    store_groups(token_out, stage)

    def part(start, height):
        return jnp.concatenate(
            [t_ref[start + c * height : start + (c + 1) * height, :] for c in range(3)], 1
        )

    def natural(kind, block):
        total = None
        for zk in range(2):
            term = dot_tn(table_rows(kind, zk), dot_nt(block, table_lanes(zk)))
            total = term if total is None else total + term
        return total

    fine_out[0:288, :] = natural("a", part(PART_A, 144))
    fine_out[288:576, :] = natural("b", part(PART_B, 80)) + natural("c", part(PART_C, 80))
    coarse_out[...] = natural("q", part(PART_Q, 288))


def mesh_parts(lat, lon):
    cores = 2
    xs = 4 if lon % 8 == 0 else 1
    ys = 4 if lat % 4 == 0 else lat
    return (cores, xs, lon // (cores * xs), ys, lat // ys)


def piece_rows(total, lon, ys):
    longest = -(-(127 + total // lon) // 128)
    unit = 16 * ys
    return -(-longest // unit) * unit


def reduce_body(
    dims,
    rows,
    norm_factor,
    g_ref,
    par_ref,
    upo_ref,
    upp_ref,
    dno_ref,
    dnp_ref,
    p_ref,
    t_ref,
    par_out,
    low_out,
    high_out,
    par_buf,
    up_buf,
    down_buf,
    up_sum,
    down_sum,
    low_buf,
    high_buf,
    ess,
    esr,
    m_head,
    m_tail,
    r1,
    r2,
    w2,
    r3,
    w3,
    r4,
    s5,
    r5,
    pf,
    tf,
    ts,
    tr,
    s1s,
    s1r,
    s2s,
    s2r,
    s3s,
    s3r,
    s4s,
    s4r,
    s5s,
    s5r,
    t4s,
    t4r,
    s6s,
    s6r,
    t6s,
    t6r,
    t7s,
    t7r,
    t8s,
    t8r,
):
    cores, xs, zs, ys, hs = dims
    chunk = rows // ys
    lat = lax.axis_index("lat")
    lon = lax.axis_index("lon")
    core = lax.rem(lon, cores)
    x = lax.rem(lon // cores, xs)
    z = lon // (cores * xs)
    y = lax.rem(lat, ys)
    h = lat // ys

    def lon_of(core_at, x_at, z_at):
        return (z_at * xs + x_at) * cores + core_at

    def core_peer():
        return (lat, lon_of(1 - core, x, z))

    def x_at(d):
        return lax.rem(x + d, xs)

    def z_at(d):
        return lax.rem(z + d, zs)

    def y_at(d):
        return lax.rem(y + d, ys)

    def x_peer(d):
        return (lat, lon_of(core, x_at(d), z))

    def z_peer(d):
        return (lat, lon_of(core, x, z_at(d)))

    def y_peer(d):
        return (h * ys + y_at(d), lon)

    def h_peer():
        return (lax.rem(h + 1, hs) * ys + y, lon)

    peers = [core_peer()]
    peers += [x_peer(d) for d in range(1, xs)]
    peers += [y_peer(d) for d in range(1, ys)]
    peers += [z_peer(d) for d in range(1, zs)]
    if hs > 1:
        peers.append(h_peer())
    lats = ys * hs
    before = (lax.rem(lat + lats - 1, lats), lon)
    after = (lax.rem(lat + 1, lats), lon)
    beside = (lat, partner_of(lon, cores * xs * zs))
    peers += [before, after, beside]
    barrier = pltpu.get_barrier_semaphore()
    for peer in peers:
        pl.semaphore_signal(barrier, inc=1, device_id=peer, device_id_type=MESH)
    pl.semaphore_wait(barrier, len(peers))

    send = start_copy
    edges = [
        send(upp_ref, up_buf, ess.at[0], esr.at[0], beside),
        send(dnp_ref, down_buf, ess.at[1], esr.at[1], beside),
        send(par_ref, par_buf, ess.at[2], esr.at[2], beside),
    ]
    pending = []
    order = (2, 1, 3, 0) if xs == 4 else (0,)
    cut = g_ref.shape[1] // 32 * 16
    head, tail = (pl.ds(0, cut), pl.ds(cut, g_ref.shape[1] - cut))
    first = {}
    for d in order:
        src = g_ref.at[pl.ds(((1 - core) * xs + x_at(d)) * zs, zs)]
        first[d] = send(src, r1.at[d], s1s.at[d], s1r.at[d], core_peer())
        pending.append(first[d])
    second = []

    def hop(at, src, dst, d):
        copy = send(src, dst, s2s.at[at], s2r.at[at], x_peer(d))
        pending.append(copy)
        return copy

    for d in order:
        first[d].wait_recv()
        base = (core * xs + x_at(d)) * zs

        def add_pair(i, carry):
            r1[d, i] = (
                r1[d, i].astype(jnp.float32) + g_ref[base + i].astype(jnp.float32)
            ).astype(jnp.bfloat16)
            return carry

        lax.fori_loop(0, zs, add_pair, 0)
        if d == 2:
            via_right = hop(0, r1.at[2, :, head], m_head, 1)
            via_left = hop(1, r1.at[2, :, tail], m_tail, 3)
        if d == 1:
            second.append(hop(2, r1.at[1, :, tail], r2.at[0, :, tail], 1))
        if d == 3:
            second.append(hop(3, r1.at[3, :, head], r2.at[1, :, head], 3))
    if xs == 4:
        via_right.wait_recv()

        def add_head(i, carry):
            r1[1, i, head, :] = (
                r1[1, i, head, :].astype(jnp.float32) + m_head[i].astype(jnp.float32)
            ).astype(jnp.bfloat16)
            return carry

        lax.fori_loop(0, zs, add_head, 0)
        second.append(hop(4, r1.at[1, :, head], r2.at[0, :, head], 1))
        via_left.wait_recv()

        def add_tail(i, carry):
            r1[3, i, tail, :] = (
                r1[3, i, tail, :].astype(jnp.float32) + m_tail[i].astype(jnp.float32)
            ).astype(jnp.bfloat16)
            return carry

        lax.fori_loop(0, zs, add_tail, 0)
        second.append(hop(5, r1.at[3, :, tail], r2.at[1, :, tail], 3))
    edges[0].wait_recv()
    edges[1].wait_recv()
    up_sum[...] = (upo_ref[...].astype(F32) + up_buf[...].astype(F32)).astype(BF16)
    down_sum[...] = (dno_ref[...].astype(F32) + down_buf[...].astype(F32)).astype(BF16)
    for copy in second:
        copy.wait_recv()

    def add_x(i, carry):
        total = r1[0, i].astype(jnp.float32)
        if xs == 4:
            total = total + r2[0, i].astype(jnp.float32) + r2[1, i].astype(jnp.float32)
        w2[i] = total.astype(jnp.bfloat16)
        return carry

    lax.fori_loop(0, zs, add_x, 0)

    third = []
    for d in range(1, ys):
        src = w2.at[:, pl.ds(pl.multiple_of(y_at(d) * chunk, 16), chunk)]
        copy = send(src, r3.at[d - 1], s3s.at[d - 1], s3r.at[d - 1], y_peer(d))
        third.append(copy)
        pending.append(copy)
    edges.append(send(up_sum, low_buf, ess.at[3], esr.at[3], after))
    edges.append(send(down_sum, high_buf, ess.at[4], esr.at[4], before))
    pending += edges
    for copy in third:
        copy.wait_recv()

    def add_y(i, carry):
        total = w2[i, pl.ds(pl.multiple_of(y * chunk, 16), chunk), :].astype(jnp.float32)
        for d in range(1, ys):
            total = total + r3[d - 1, i].astype(jnp.float32)
        w3[i, 0:chunk, :] = total.astype(jnp.bfloat16)
        w3[i, chunk:, :] = w2[i, rows:, :]
        return carry

    lax.fori_loop(0, zs, add_y, 0)

    fourth = []
    for d in range(1, zs):
        copy = send(w3.at[z_at(d)], r4.at[d - 1], s4s.at[d - 1], s4r.at[d - 1], z_peer(d))
        fourth.append(copy)
        pending.append(copy)
    for copy in fourth:
        copy.wait_recv()
    total = w3[z].astype(jnp.float32)
    for d in range(1, zs):
        total = total + r4[d - 1].astype(jnp.float32)

    s5[...] = total[:chunk].astype(jnp.bfloat16)
    if hs > 1:
        fifth = send(s5, r5, s5s.at[0], s5r.at[0], h_peer())
        pending.append(fifth)
    ts[...] = (total[chunk:] * norm_factor).astype(jnp.bfloat16)
    first_row = ((core * xs + x) * zs + z) * ts.shape[0]
    handed = pltpu.make_async_remote_copy(
        src_ref=ts,
        dst_ref=tr,
        send_sem=t8s.at[0],
        recv_sem=t8r.at[0],
        device_id=before,
        device_id_type=MESH,
    )
    tf[core, x, z] = ts[...]

    @pl.when(first_row < PART_A)
    def _():
        handed.start()
        handed.wait_recv()
        row = first_row + lax.broadcasted_iota(jnp.int32, ts.shape, 0)
        tf[core, x, z] = jnp.where(
            row < PART_A, tr[...].astype(jnp.float32), ts[...].astype(jnp.float32)
        ).astype(jnp.bfloat16)
        handed.wait_send()

    table_z = []
    for d in range(1, zs):
        copy = send(
            tf.at[core, x, z], tf.at[core, x, z], t4s.at[d - 1], t4r.at[d - 1], z_peer(d)
        )
        table_z.append(copy)
        pending.append(copy)
    share = s5[...].astype(jnp.float32)
    if hs > 1:
        fifth.wait_recv()
        share = share + r5[...].astype(jnp.float32)
    mine = pl.ds(pl.multiple_of(y * chunk, 8), chunk)
    pf[mine, :] = share * norm_factor
    sixth = []
    for d in range(1, ys):
        copy = send(pf.at[mine], pf.at[mine], s6s.at[d - 1], s6r.at[d - 1], y_peer(d))
        sixth.append(copy)
        pending.append(copy)
    for copy in table_z:
        copy.wait_recv()
    table_x = []
    for d in range(1, xs):
        copy = send(tf.at[core, x], tf.at[core, x], t6s.at[d - 1], t6r.at[d - 1], x_peer(d))
        table_x.append(copy)
        pending.append(copy)
    for copy in table_x:
        copy.wait_recv()
    table_core = send(tf.at[core], tf.at[core], t7s.at[0], t7r.at[0], core_peer())
    pending.append(table_core)
    for copy in sixth:
        copy.wait_recv()
    p_ref[...] = pf[...]
    for copy in edges[2:]:
        copy.wait_recv()
    par_out[...] = par_buf[...]
    low_out[...] = low_buf[...]
    high_out[...] = high_buf[...]
    table_core.wait_recv()
    t_ref[...] = tf[...]
    for copy in pending:
        copy.wait_send()


def reduce_all(pieces, edges, rows, norm_factor, dims):
    cores, xs, zs, ys, hs = dims
    height = pieces.shape[1]
    trows = height - rows
    chunk = rows // ys
    bf16 = jnp.bfloat16
    sem = pltpu.SemaphoreType.DMA
    cut = height // 32 * 16
    counts = [xs, 6, ys - 1, zs - 1, 1, zs - 1, ys - 1, xs - 1, 1, 1]
    sems = []
    for count in counts:
        sems += [sem((max(count, 1),)), sem((max(count, 1),))]
    vmem = pl.BlockSpec(memory_space=pltpu.VMEM)
    return pl.pallas_call(
        functools.partial(reduce_body, dims, rows, norm_factor),
        out_shape=(
            jax.ShapeDtypeStruct((rows, 128), jnp.float32),
            jax.ShapeDtypeStruct((cores, xs, zs, trows, 128), bf16),
            jax.ShapeDtypeStruct((FINE, C_F), bf16),
            jax.ShapeDtypeStruct((128, 128), bf16),
            jax.ShapeDtypeStruct((128, 128), bf16),
        ),
        in_specs=[vmem] * 6,
        out_specs=(vmem,) * 5,
        scratch_shapes=[pltpu.VMEM((FINE, C_F), bf16)]
        + [pltpu.VMEM((128, 128), bf16)] * 6
        + [sem((5,)), sem((5,))]
        + [pltpu.VMEM((zs, cut, 128), bf16), pltpu.VMEM((zs, height - cut, 128), bf16)]
        + [
            pltpu.VMEM((xs, zs, height, 128), bf16),
            pltpu.VMEM((2, zs, height, 128), bf16),
            pltpu.VMEM((zs, height, 128), bf16),
            pltpu.VMEM((max(ys - 1, 1), zs, chunk, 128), bf16),
            pltpu.VMEM((zs, chunk + trows, 128), bf16),
            pltpu.VMEM((max(zs - 1, 1), chunk + trows, 128), bf16),
            pltpu.VMEM((chunk, 128), bf16),
            pltpu.VMEM((chunk, 128), bf16),
            pltpu.VMEM((rows, 128), jnp.float32),
            pltpu.VMEM((cores, xs, zs, trows, 128), bf16),
            pltpu.VMEM((trows, 128), bf16),
            pltpu.VMEM((trows, 128), bf16),
        ]
        + sems,
        compiler_params=pltpu.CompilerParams(
            collective_id=7, has_side_effects=True, vmem_limit_bytes=VMEM_BYTES
        ),
        cost_estimate=lasting(45),
        name="grad_reduce",
    )(pieces, *edges)


def shards(
    tokens,
    fine_gain,
    fine_shift,
    fine_qkv,
    fine_qkv_bias,
    fine_proj,
    fine_proj_bias,
    fine_table,
    merge_gain,
    merge_shift,
    merge_weight,
    coarse_gain,
    coarse_shift,
    coarse_qkv,
    coarse_qkv_bias,
    coarse_proj,
    coarse_proj_bias,
    coarse_table,
    cotangent,
):
    lat_count, lon_count = (lax.axis_size("lat"), lax.axis_size("lon"))
    lat, lon = (lax.axis_index("lat"), lax.axis_index("lon"))
    norm_factor = 1.0 / math.sqrt(tokens.size // C_F * lat_count * lon_count / 4)
    fine_rows = fine_table.reshape(576, 138)
    coarse_rows = coarse_table.reshape(576, 138)
    cells = tokens[0].transpose(1, 2, 0, 3)
    cot_cells = cotangent[0].transpose(1, 2, 0, 3)

    group = min(8, lon_count)
    side = ((128, 128), BF16)
    own = ((FINE, C_F), BF16)
    table_part = ((group, PART_A // group, 128), BF16)
    x, low, high, table_send = call(
        prepare_body,
        [own, side, side, table_part],
        (cells, fine_rows),
        [pltpu.VMEM((288, C_F), F32)],
        "prepare",
        2,
    )
    halo = [own, side, side, side, side, table_part]
    par, upo, upp, dno, dnp, table_before = exchange_call(
        halo_body,
        halo,
        (x, low, high, table_send),
        [pltpu.VMEM(*s) for s in halo],
        (6, max(group - 1, 1)),
        1,
        "halo",
        10,
    )
    (
        hat,
        normed,
        q,
        k,
        v,
        probs_a,
        probs_b,
        probs_c,
        mixture,
        fine_out,
        merged,
        coarse,
        cnorm,
    ) = call(
        fine_forward_body,
        [
            ((ALL_ROWS, C_F), F32),
            ((ALL_ROWS, C_F), BF16),
            ((FINE, C_F), F32),
            ((ALL_ROWS, C_F), F32),
            ((ALL_ROWS, C_F), F32),
            ((2, 432, 144), F32),
            ((2, 240, 160), F32),
            ((2, 240, 160), F32),
            own,
            own,
            ((4, COARSE, C_F), BF16),
            ((COARSE, C_C), F32),
            ((COARSE, C_C), BF16),
        ],
        (
            x,
            par,
            upo,
            upp,
            dno,
            dnp,
            fine_gain,
            fine_shift,
            fine_qkv,
            fine_qkv_bias,
            fine_proj,
            fine_proj_bias,
            merge_gain,
            merge_shift,
            merge_weight,
            coarse_gain,
            coarse_shift,
            fine_rows,
            table_before.reshape(PART_A, 128),
        ),
        (),
        "fine_forward",
        10,
    )
    gathered_to = [((4, COARSE, C_C), BF16)]
    (gathered_norm,) = exchange_call(
        group_body, gathered_to, (cnorm,), [pltpu.VMEM(*gathered_to[0])], (3,), 2, "coarse_gather", 5
    )
    coarse_out, parts, own_part, flat_c, table_q, cot = call(
        coarse_body,
        [
            ((6, 3, 4, C_C), BF16),
            ((4, COARSE, C_C), BF16),
            ((COARSE, C_C), F32),
            ((4620, 128), F32),
            ((288, 384), F32),
            ((COARSE, C_C), F32),
        ],
        (
            gathered_norm,
            cnorm,
            coarse,
            cot_cells,
            coarse_qkv,
            coarse_qkv_bias,
            coarse_proj,
            coarse_proj_bias,
            coarse_rows,
        ),
        [
            pltpu.VMEM((72, C_C), F32),
            pltpu.VMEM((4 * COARSE, C_C), F32),
            pltpu.VMEM((4 * COARSE, C_C), F32),
        ],
        "coarse_attention",
        7,
    )
    (norm_part,) = exchange_call(
        ungroup_body,
        [((COARSE, C_C), F32)],
        (parts,),
        [pltpu.VMEM((3, COARSE, C_C), BF16)],
        (3,),
        3,
        "coarse_scatter",
        5,
    )
    dims = mesh_parts(lat_count, lon_count)
    cores, xs, zs, ys, hs = dims
    segment = PARAMS // lon_count
    rows = piece_rows(PARAMS, lon_count, ys)
    starts = []
    for index in range(lon_count):
        core, x_at, z_at = (index % cores, index // cores % xs, index // (cores * xs))
        starts.append(((core * xs + x_at) * zs + z_at, index * segment // 128))
    trows = TABLE_ROWS // lon_count
    fine_out_grad, own_grad, par_grad, upo_grad, upp_grad, dno_grad, dnp_grad, pieces = call(
        functools.partial(fine_back_body, starts, rows),
        [
            ((FINE, C_F), F32),
            ((FINE, C_F), F32),
            own,
            side,
            side,
            side,
            side,
            ((lon_count, rows + trows, 128), BF16),
        ],
        (
            norm_part,
            own_part,
            cot,
            coarse,
            merged,
            fine_out,
            hat,
            normed,
            mixture,
            q,
            k,
            v,
            probs_a,
            probs_b,
            probs_c,
            fine_qkv,
            coarse_gain,
            merge_gain,
            merge_weight,
            fine_proj,
            flat_c,
            table_q,
        ),
        [
            pltpu.VMEM((ALL_ROWS, C_F), F32),
            pltpu.VMEM((ALL_ROWS, C_F), F32),
            pltpu.VMEM((3488, 128), F32),
            pltpu.VMEM((TABLE_ROWS, 128), F32),
            pltpu.VMEM((2, 200, 128), F32),
        ],
        "fine_backward",
        9,
    )
    owned, table_sum, par_back, low_back, high_back = reduce_all(
        pieces, (par_grad, upo_grad, upp_grad, dno_grad, dnp_grad), rows, norm_factor, dims
    )
    shift = lax.rem(lon * segment, 128)
    param_grads = lax.dynamic_slice(owned.reshape(-1), (shift,), (segment,))
    token_grad, fine_total, coarse_total = call(
        final_body,
        [((12, 6, 4, C_F), BF16), ((576, 138), F32), ((576, 138), F32)],
        (
            x,
            fine_gain,
            fine_out_grad,
            own_grad,
            par_back,
            low_back,
            high_back,
            table_sum.reshape(TABLE_ROWS, 128),
        ),
        [pltpu.VMEM((288, C_F), F32), pltpu.VMEM((FINE, C_F), F32)],
        "final",
        2,
    )
    return (
        coarse_out.transpose(2, 0, 1, 3)[None],
        token_grad.transpose(2, 0, 1, 3)[None],
        param_grads,
        fine_total.reshape(2, -1),
        coarse_total.reshape(2, -1),
    )


def solution(mesh):
    tiles = P(None, None, "lat", "lon", None)
    whole = P()
    rows = P("lat", None)
    return jax.shard_map(
        shards,
        mesh=mesh,
        in_specs=(tiles,) + (whole,) * 6 + (rows,) + (whole,) * 9 + (rows, tiles),
        out_specs=(tiles, tiles, P("lon"), rows, rows),
        check_vma=False,
    )
```

profile of v0, /device:TPU:29, one launch (start us, length us, event | category | flops | bytes accessed | tf_op | source)
XLA Modules:
  0.0 159.7 jit_solution(6195702240250168781)
XLA Ops:
  0.6 0.0 copy-start
  0.6 2.5 %reshape.31.tf_ref = bf16[576,138]{1,0:T(8,128)(2,1)} reshape(bf16[2,39744]{1,0:T(2,128)(2,1)} %param.26) | data formatting | bytes 317952 | tf_op jit(solution)/shard_map/reshape | solution.py:1264
  3.1 2.5 %prepare.1 = (bf16[304,192]{1,0:T(8,128)(2,1)}, bf16[128,128]{1,0:T(8,128)(2,1)}, bf16[128,128]{1,0:T(8,128)(2,1)}, bf16[8,32,128]{2,1,0:T(8,128)(2,1)}) custom-call(bf16[12,6,4,192]{3,2,1,0:T(4,128)(2,1)} %bitcast.16, bf16[576,138]{1,0:T(8,128)(2,1)} %reshape.31.tf_ref), custom_call_target="tpu_custom_call" | custom-call | bytes 7380000 | tf_op jit(solution)/shard_map/prepare/pallas_call | solution.py:245
  5.6 27.6 %halo.1 = (bf16[304,192]{1,0:T(8,128)(2,1)}, bf16[128,128]{1,0:T(8,128)(2,1)}, bf16[128,128]{1,0:T(8,128)(2,1)}, bf16[128,128]{1,0:T(8,128)(2,1)}, bf16[128,128]...) custom-call(bf16[304,192]{1,0:T(8,128)(2,1)} %get-tuple-element.50.x_ref.own_ref, bf16[128,128]{1,0:T(8,128)(2,1)} %get-tuple-element.51.low_ref, ...), custom_call_target="tpu_custom_call" | custom-call | bytes 36900000 | tf_op jit(solution)/shard_map/halo/pallas_call | solution.py:328
  33.3 10.3 %fine_forward.1 = (f32[928,192]{1,0:T(8,128)}, bf16[928,192]{1,0:T(8,128)(2,1)}, f32[304,192]{1,0:T(8,128)}, f32[928,192]{1,0:T(8,128)}, f32[928,192]{1,0:T(8,12...) custom-call(bf16[304,192]{1,0:T(8,128)(2,1)} %get-tuple-element.50.x, ...), custom_call_target="tpu_custom_call" | custom-call | bytes 36900000 | tf_op jit(solution)/shard_map/fine_forward/pallas_call | solution.py:245
  43.6 7.7 %coarse_gather.1.group_ref = bf16[4,80,384]{2,1,0:T(8,128)(2,1)} custom-call(bf16[80,384]{1,0:T(8,128)(2,1)} %get-tuple-element.60.own_ref), custom_call_target="tpu_custom_call" | custom-call | bytes 18450000 | tf_op jit(solution)/shard_map/coarse_gather/pallas_call | solution.py:328
  51.2 0.0 copy-done
  51.2 1.6 reshape.33.tc_ref
  52.8 10.0 %coarse_attention.1 = (bf16[6,3,4,384]{3,2,1,0:T(4,128)(2,1)}, bf16[4,80,384]{2,1,0:T(8,128)(2,1)}, f32[80,384]{1,0:T(8,128)}, f32[4620,128]{1,0:T(8,128)}, f32[288,384]{1,0:T(8,128)}, /*index=5*/f32[80,384]{1,0:T(8,128)}) custom-call(bf16[4,80,384]{2,1,0:T(8,128)(2,1)} %coarse_gather.1.group_ref, bf16[80,384]{1,0:T(8,128)(2,1)} %get-tuple-element.60.own_ref, ...), custom_call_target="tpu_custom_call" | custom-call | bytes 25830000 | tf_op jit(solution)/shard_map/coarse_attention/pallas_call | solution.py:245
  62.9 7.5 %coarse_scatter.1.part_ref = f32[80,384]{1,0:T(8,128)} custom-call(bf16[4,80,384]{2,1,0:T(8,128)(2,1)} %get-tuple-element.63.parts_ref), custom_call_target="tpu_custom_call" | custom-call | bytes 18450000 | tf_op jit(solution)/shard_map/coarse_scatter/pallas_call | solution.py:328
  70.3 14.0 %fine_backward.1 = (f32[304,192]{1,0:T(8,128)}, f32[304,192]{1,0:T(8,128)}, bf16[304,192]{1,0:T(8,128)(2,1)}, bf16[128,128]{1,0:T(8,128)(2,1)}, bf16[128,128]{1,...) custom-call(f32[80,384]{1,0:T(8,128)} %coarse_scatter.1.part_ref, ...), custom_call_target="tpu_custom_call" | custom-call | bytes 33210000 | tf_op jit(solution)/shard_map/fine_backward/pallas_call | solution.py:245
  84.4 64.2 %grad_reduce.1 = (f32[128,128]{1,0:T(8,128)}, bf16[2,4,8,32,128]{4,3,2,1,0:T(8,128)(2,1)}, bf16[304,192]{1,0:T(8,128)(2,1)}, bf16[128,128]{1,0:T(8,128)(2,1)}, bf16[128,128]{1,0:T(8,128)(2,1)}) custom-call(bf16[64,160,128]{2,1,0:T(8,128)(2,1)} %get-tuple-element.81.g_ref, bf16[304,192]{1,0:T(8,128)(2,1)} %get-tuple-element.82.par_ref, ...), custom_call_target="tpu_custom_call" | custom-call | bytes 166050000 | tf_op jit(solution)/shard_map/grad_reduce/pallas_call | solution.py:1202
  148.6 4.7 %final.1 = (bf16[12,6,4,192]{3,2,1,0:T(4,128)(2,1)}, f32[576,138]{1,0:T(8,128)}, f32[576,138]{1,0:T(8,128)}) custom-call(bf16[304,192]{1,0:T(8,128)(2,1)} %get-tuple-element.50.x_ref.own_ref, f32[192]{0:T(256)} %gain_ref.3, f32[304,192]{1,0:T(8,128)} %get-tuple-element.79.fog_ref, f32[304,192]{1,0:T(8,128)} %get-tuple-element.80.own_ref, ...), custom_call_target="tpu_custom_call" | custom-call | bytes 7380000 | tf_op jit(solution)/shard_map/final/pallas_call | solution.py:245
  153.3 1.6 dynamic_slice.3
  154.8 2.4 %reshape.36 = f32[2,39744]{1,0:T(2,128)} reshape(f32[576,138]{1,0:T(8,128)} %get-tuple-element.93) | data formatting | bytes 635904 | tf_op jit(solution)/shard_map/reshape | solution.py:1472
  157.3 2.4 %reshape.37 = f32[2,39744]{1,0:T(2,128)} reshape(f32[576,138]{1,0:T(8,128)} %get-tuple-element.94) | data formatting | bytes 635904 | tf_op jit(solution)/shard_map/reshape | solution.py:1473
Async XLA Ops:
  0.6 50.6 %copy-start = (bf16[2,39744]{1,0:T(2,128)(2,1)S(1)}, bf16[2,39744]{1,0:T(2,128)(2,1)}, u32[]{:S(2)}) copy-start(bf16[2,39744]{1,0:T(2,128)(2,1)} %param.36) | copy-start | bytes 476932
where the time goes:
time: 160 us
  Pallas kernels  149 us (93%)
  local copies, waits for them, and re-layouts  10.5 us (7%)
    pallas_call x1, Pallas kernels, reduce_all(): pl.pallas_call(functools.partial(reduce_body, dims, rows, norm_factor), o...  64.2 us
    pallas_call x3, Pallas kernels, exchange_call(): pl.pallas_call(body, out_shape=tuple((jax.ShapeDtypeStruct(shape, dtype)...  42.8 us
    pallas_call x5, Pallas kernels, call(): pl.pallas_call(body, out_shape=tuple((jax.ShapeDtypeStruct(shape, dtype)...  41.6 us

commit v1 on v0

--- a/solution.py
+++ b/solution.py
@@ -20,7 +20,7 @@
 F32 = jnp.float32
 BF16 = jnp.bfloat16
 MIB = 1024 * 1024
-VMEM_BYTES = 60 * MIB
+VMEM_BYTES = 28 * MIB
 
 LOW, MID, TOP = (0, 80, 224)
 PARAMS = 1037184
@@ -236,7 +236,7 @@
 
 
 def lasting(micros):
-    return pl.CostEstimate(flops=0, bytes_accessed=int(micros * 3.69e6), transcendentals=0)
+    return pl.CostEstimate(flops=int(micros * 2.0e9), bytes_accessed=int(micros * 3.69e6), transcendentals=int(micros * 1e6))
 
 
 def call(body, outs, args, scratch, name, micros, in_place=(), limit=VMEM_BYTES):
@@ -457,6 +457,33 @@
     return {"a": mid, "b": edge, "c": edge}
 
 
+def bias_body(tf_ref, tp_ref, tc_ref, out_a, out_b, out_c, out_q):
+    tables = {
+        "a": spread("a", tf_ref[0:288, :]),
+        "b": spread("b", tf_ref[288:576, :]),
+        "c": jnp.concatenate([tp_ref[c * 80 : (c + 1) * 80, :].astype(F32) for c in range(3)], 1),
+    }
+    lat = lax.axis_index("lat")
+    late = along_lanes(160) >= 80
+    edges = {
+        "a": 0.0,
+        "b": jnp.where(late & (lat == lax.axis_size("lat") - 1), NEGATIVE, 0.0),
+        "c": jnp.where(jnp.logical_not(late) & (lat == 0), NEGATIVE, 0.0),
+    }
+    kinds = fine_kinds()
+    for name, out in (("a", out_a), ("b", out_b), ("c", out_c)):
+        _, _, zq, keys, toep, block = kinds[name]
+        for zone in range(2):
+            terms = bias_rows(tables[name], toep, zone, block)
+            out[zone] = terms + banned(keys, zq, zone) + edges[name]
+    _, _, zq = head_rows(HEADS_C, 6, 3, 40, 144)
+    cells = group_keys()
+    toep = toeplitz(cells, 3, 3 * lax.rem(lax.axis_index("lon"), 4).astype(F32))
+    table = spread("q", tc_ref[...])
+    for zone in range(2):
+        out_q[zone] = bias_rows(table, toep, zone, 144) + banned(cells, zq, 0)
+
+
 def fine_windows(zone):
     edge = zone * 40
     return (
@@ -495,8 +522,9 @@
     merge_ref,
     coarse_gain_ref,
     coarse_shift_ref,
-    tf_ref,
-    tp_ref,
+    bias_a,
+    bias_b,
+    bias_c,
     hat_out,
     normed,
     q_out,
@@ -525,33 +553,20 @@
     q_out[...] = rounded(dot(normed[0:FINE, :], qkv_ref[:, 0:C_F]) + bias[:, 0:C_F])
     k_out[...] = rounded(dot(normed[...], qkv_ref[:, C_F : 2 * C_F]) + bias[:, C_F : 2 * C_F])
     v_out[...] = rounded(dot(normed[...], qkv_ref[:, 2 * C_F :]) + bias[:, 2 * C_F :])
-    tables = {
-        "a": spread("a", tf_ref[0:288, :]),
-        "b": spread("b", tf_ref[288:576, :]),
-        "c": jnp.concatenate([tp_ref[c * 80 : (c + 1) * 80, :].astype(F32) for c in range(3)], 1),
-    }
-    lat = lax.axis_index("lat")
-    late = along_lanes(160) >= 80
-    edges = {
-        "a": 0.0,
-        "b": jnp.where(late & (lat == lax.axis_size("lat") - 1), NEGATIVE, 0.0),
-        "c": jnp.where(jnp.logical_not(late) & (lat == 0), NEGATIVE, 0.0),
-    }
     kinds = fine_kinds()
-    probs_refs = {"a": probs_a, "b": probs_b, "c": probs_c}
+    probs_refs = {"a": (bias_a, probs_a), "b": (bias_b, probs_b), "c": (bias_c, probs_c)}
     mixtures = {}
     for zone in range(2):
         for name, (start, count), pieces in fine_windows(zone):
-            rows, mask, zq, keys, toep, block = kinds[name]
-            probs_ref = probs_refs[name]
-            bias = bias_rows(tables[name], toep, zone, block) + banned(keys, zq, zone) + edges[name]
+            rows, mask = kinds[name][:2]
+            bias_ref, probs_ref = probs_refs[name]
             probs, mixture = attend(
                 q_out[start : start + count, :],
                 gathered(k_out, pieces),
                 gathered(v_out, pieces),
                 rows,
                 mask,
-                bias,
+                bias_ref[zone],
             )
             probs_ref[zone] = probs
             mixtures[name, zone] = mixture
@@ -595,7 +610,7 @@
     qkv_bias_ref,
     proj_ref,
     proj_bias_ref,
-    tc_ref,
+    bias_ref,
     out_ref,
     parts_out,
     own_out,
@@ -617,18 +632,15 @@
     keys[...] = rounded(dot(group, qkv_ref[:, wide[1]]) + bias[:, wide[1]])
     values[...] = rounded(dot(group, qkv_ref[:, wide[2]]) + bias[:, wide[2]])
     mixture_grad = rounded(dot_nt(cot, proj_ref[...]))
-    rows, mask, zq = head_rows(HEADS_C, 6, 3, 40, 144)
-    cells = group_keys()
-    toep = toeplitz(cells, 3, 3 * lax.rem(lax.axis_index("lon"), 4).astype(F32))
-    table_in = spread("q", tc_ref[...])
+    rows, mask, _ = head_rows(HEADS_C, 6, 3, 40, 144)
+    toep = toeplitz(group_keys(), 3, 3 * lax.rem(lax.axis_index("lon"), 4).astype(F32))
     mixtures, query_grads, grads = ([], [], [])
     for zone in range(2):
         here = slice(zone * 40, (zone + 1) * 40)
         at = [slice(g * COARSE + zone * 40, g * COARSE + zone * 40 + 40) for g in range(4)]
         k = jnp.concatenate([keys[there, :] for there in at], 0)
         v = jnp.concatenate([values[there, :] for there in at], 0)
-        bias = bias_rows(table_in, toep, zone, 144) + banned(cells, zq, 0)
-        probs, mixture = attend(queries[here], k, v, rows, mask, bias)
+        probs, mixture = attend(queries[here], k, v, rows, mask, bias_ref[zone])
         dq, dk, dv, table = attend_back(
             queries[here], k, v, rows, mask, probs, mixture_grad[here], toep, 144
         )
@@ -729,6 +741,7 @@
     dno_out,
     dnp_out,
     pieces_out,
+    tables_out,
     kgrad,
     vgrad,
     flat,
@@ -838,8 +851,10 @@
             value = flat_c[start - split : start - split + size, :]
             if size < rows:
                 value = jnp.concatenate([value, jnp.zeros((rows - size, 128), F32)], 0)
-        pieces_out[place, 0:rows, :] = value.astype(BF16)
-        pieces_out[place, rows:, :] = tables[place * trows : (place + 1) * trows, :].astype(BF16)
+        chunk = pieces_out.shape[2]
+        for y in range(pieces_out.shape[0]):
+            pieces_out[y, place] = value[y * chunk : (y + 1) * chunk].astype(BF16)
+        tables_out[place] = tables[place * trows : (place + 1) * trows, :].astype(BF16)
 
 
 def final_body(
@@ -897,9 +912,9 @@
 
 def reduce_body(
     dims,
-    rows,
     norm_factor,
     g_ref,
+    gt_ref,
     par_ref,
     upo_ref,
     upp_ref,
@@ -917,324 +932,265 @@
     down_sum,
     low_buf,
     high_buf,
-    ess,
-    esr,
-    m_head,
-    m_tail,
-    r1,
-    r2,
-    w2,
-    r3,
-    w3,
-    r4,
-    s5,
-    r5,
-    pf,
-    tf,
-    ts,
-    tr,
-    s1s,
-    s1r,
-    s2s,
-    s2r,
-    s3s,
-    s3r,
-    s4s,
-    s4r,
-    s5s,
-    s5r,
-    t4s,
-    t4r,
-    s6s,
-    s6r,
-    t6s,
-    t6r,
-    t7s,
-    t7r,
-    t8s,
-    t8r,
+    core_buf,
+    head_buf,
+    tail_buf,
+    y_buf,
+    y_sum,
+    x_buf,
+    x_sum,
+    z_buf,
+    h_send,
+    h_buf,
+    share,
+    tab_core,
+    tab_x,
+    tab_sum,
+    tab_hand,
+    tab_z,
+    tab_all,
+    send_sems,
+    recv_sems,
 ):
     cores, xs, zs, ys, hs = dims
-    chunk = rows // ys
-    lat = lax.axis_index("lat")
-    lon = lax.axis_index("lon")
+    half = xs * zs
+    chunk = g_ref.shape[2]
+    trows = gt_ref.shape[1]
+    lat, lon = (lax.axis_index("lat"), lax.axis_index("lon"))
     core = lax.rem(lon, cores)
     x = lax.rem(lon // cores, xs)
     z = lon // (cores * xs)
     y = lax.rem(lat, ys)
     h = lat // ys
-
-    def lon_of(core_at, x_at, z_at):
-        return (z_at * xs + x_at) * cores + core_at
-
-    def core_peer():
-        return (lat, lon_of(1 - core, x, z))
-
-    def x_at(d):
-        return lax.rem(x + d, xs)
-
-    def z_at(d):
-        return lax.rem(z + d, zs)
-
-    def y_at(d):
-        return lax.rem(y + d, ys)
-
-    def x_peer(d):
-        return (lat, lon_of(core, x_at(d), z))
-
-    def z_peer(d):
-        return (lat, lon_of(core, x, z_at(d)))
-
-    def y_peer(d):
-        return (h * ys + y_at(d), lon)
-
-    def h_peer():
-        return (lax.rem(h + 1, hs) * ys + y, lon)
-
-    peers = [core_peer()]
-    peers += [x_peer(d) for d in range(1, xs)]
-    peers += [y_peer(d) for d in range(1, ys)]
-    peers += [z_peer(d) for d in range(1, zs)]
+    lats = ys * hs
+
+    def at(here, d, count):
+        return lax.rem(here + d, count)
+
+    def lon_of(core_to, x_to, z_to):
+        return (z_to * xs + x_to) * cores + core_to
+
+    other_core = (lat, lon_of(1 - core, x, z))
+    x_peers = {d: (lat, lon_of(core, at(x, d, xs), z)) for d in range(1, xs)}
+    y_peers = {d: (h * ys + at(y, d, ys), lon) for d in range(1, ys)}
+    z_peers = {d: (lat, lon_of(core, x, at(z, d, zs))) for d in range(1, zs)}
+    far = (at(h, 1, hs) * ys + y, lon)
+    before, after = ((at(lat, lats - 1, lats), lon), (at(lat, 1, lats), lon))
+    beside = (lat, partner_of(lon, cores * half))
+    peers = [other_core, before, after, beside]
+    peers += list(x_peers.values()) + list(y_peers.values()) + list(z_peers.values())
     if hs > 1:
-        peers.append(h_peer())
-    lats = ys * hs
-    before = (lax.rem(lat + lats - 1, lats), lon)
-    after = (lax.rem(lat + 1, lats), lon)
-    beside = (lat, partner_of(lon, cores * xs * zs))
-    peers += [before, after, beside]
-    barrier = pltpu.get_barrier_semaphore()
-    for peer in peers:
-        pl.semaphore_signal(barrier, inc=1, device_id=peer, device_id_type=MESH)
-    pl.semaphore_wait(barrier, len(peers))
-
-    send = start_copy
-    edges = [
-        send(upp_ref, up_buf, ess.at[0], esr.at[0], beside),
-        send(dnp_ref, down_buf, ess.at[1], esr.at[1], beside),
-        send(par_ref, par_buf, ess.at[2], esr.at[2], beside),
-    ]
+        peers.append(far)
+    meet(peers)
     pending = []
-    order = (2, 1, 3, 0) if xs == 4 else (0,)
-    cut = g_ref.shape[1] // 32 * 16
-    head, tail = (pl.ds(0, cut), pl.ds(cut, g_ref.shape[1] - cut))
-    first = {}
-    for d in order:
-        src = g_ref.at[pl.ds(((1 - core) * xs + x_at(d)) * zs, zs)]
-        first[d] = send(src, r1.at[d], s1s.at[d], s1r.at[d], core_peer())
-        pending.append(first[d])
-    second = []
-
-    def hop(at, src, dst, d):
-        copy = send(src, dst, s2s.at[at], s2r.at[at], x_peer(d))
+
+    def send(src, dst, peer):
+        sem = len(pending)
+        copy = start_copy(src, dst, send_sems.at[sem], recv_sems.at[sem], peer)
         pending.append(copy)
         return copy
 
+    def arrived(copies):
+        for copy in copies:
+            copy.wait_recv()
+
+    def add_into(target, terms, count):
+        def step(i, carry):
+            total = terms[0](i).astype(F32)
+            for term in terms[1:]:
+                total = total + term(i).astype(F32)
+            target[i] = total.astype(BF16)
+            return carry
+
+        lax.fori_loop(0, count, step, 0)
+
+    away = pl.ds((1 - core) * half, half)
+    mine = core * half
+    table_core = send(gt_ref.at[away], tab_core, other_core)
+    edges = [
+        send(upp_ref, up_buf, beside),
+        send(dnp_ref, down_buf, beside),
+        send(par_ref, par_buf, beside),
+    ]
+    order = {4: (2, 1, 3, 0), 2: (1, 0), 1: (0,)}[ys]
+    crossing = {d: send(g_ref.at[at(y, d, ys), away], core_buf.at[d], other_core) for d in order}
+    table_core.wait_recv()
+    add_into(tab_core, [lambda i: tab_core[i], lambda i: gt_ref[mine + i]], half)
+    table_x = [
+        send(tab_core.at[pl.ds(at(x, d, xs) * zs, zs)], tab_x.at[d - 1], x_peers[d])
+        for d in range(1, xs)
+    ]
+    cut = half // 2
+    head, tail = (pl.ds(0, cut), pl.ds(cut, half - cut))
+    gathered_y = []
     for d in order:
-        first[d].wait_recv()
-        base = (core * xs + x_at(d)) * zs
-
-        def add_pair(i, carry):
-            r1[d, i] = (
-                r1[d, i].astype(jnp.float32) + g_ref[base + i].astype(jnp.float32)
-            ).astype(jnp.bfloat16)
-            return carry
-
-        lax.fori_loop(0, zs, add_pair, 0)
-        if d == 2:
-            via_right = hop(0, r1.at[2, :, head], m_head, 1)
-            via_left = hop(1, r1.at[2, :, tail], m_tail, 3)
-        if d == 1:
-            second.append(hop(2, r1.at[1, :, tail], r2.at[0, :, tail], 1))
-        if d == 3:
-            second.append(hop(3, r1.at[3, :, head], r2.at[1, :, head], 3))
-    if xs == 4:
-        via_right.wait_recv()
-
-        def add_head(i, carry):
-            r1[1, i, head, :] = (
-                r1[1, i, head, :].astype(jnp.float32) + m_head[i].astype(jnp.float32)
-            ).astype(jnp.bfloat16)
-            return carry
-
-        lax.fori_loop(0, zs, add_head, 0)
-        second.append(hop(4, r1.at[1, :, head], r2.at[0, :, head], 1))
-        via_left.wait_recv()
-
-        def add_tail(i, carry):
-            r1[3, i, tail, :] = (
-                r1[3, i, tail, :].astype(jnp.float32) + m_tail[i].astype(jnp.float32)
-            ).astype(jnp.bfloat16)
-            return carry
-
-        lax.fori_loop(0, zs, add_tail, 0)
-        second.append(hop(5, r1.at[3, :, tail], r2.at[1, :, tail], 3))
-    edges[0].wait_recv()
-    edges[1].wait_recv()
+        crossing[d].wait_recv()
+        row = at(y, d, ys)
+        buf = core_buf.at[d]
+        add_into(buf, [lambda i: buf[i], lambda i: g_ref[row, mine + i]], half)
+        if ys == 4 and d == 2:
+            over_right = send(core_buf.at[2, head], head_buf, y_peers[1])
+            over_left = send(core_buf.at[2, tail], tail_buf, y_peers[3])
+        if ys == 4 and d == 1:
+            gathered_y.append(send(core_buf.at[1, tail], y_buf.at[0, tail], y_peers[1]))
+        if ys == 4 and d == 3:
+            gathered_y.append(send(core_buf.at[3, head], y_buf.at[1, head], y_peers[3]))
+        if ys == 2 and d == 1:
+            gathered_y.append(send(core_buf.at[1], y_buf.at[0], y_peers[1]))
+    if ys == 4:
+        over_right.wait_recv()
+        right = core_buf.at[1]
+        add_into(right, [lambda i: right[i], lambda i: head_buf[i]], cut)
+        gathered_y.append(send(core_buf.at[1, head], y_buf.at[0, head], y_peers[1]))
+        over_left.wait_recv()
+        left = core_buf.at[3, tail]
+        add_into(left, [lambda i: left[i], lambda i: tail_buf[i]], half - cut)
+        gathered_y.append(send(core_buf.at[3, tail], y_buf.at[1, tail], y_peers[3]))
+
+    arrived(table_x)
+    base = x * zs
+    terms = [lambda i: tab_core[base + i]]
+    terms += [lambda i, d=d: tab_x[d - 1, i] for d in range(1, xs)]
+    add_into(tab_sum, terms, zs)
+    first_row = (core * xs + x) * zs * trows
+    hand_sem = len(pending)
+    handed = pltpu.make_async_remote_copy(
+        src_ref=tab_sum,
+        dst_ref=tab_hand,
+        send_sem=send_sems.at[hand_sem],
+        recv_sem=recv_sems.at[hand_sem],
+        device_id=before,
+        device_id_type=MESH,
+    )
+    arrived(edges[:2])
     up_sum[...] = (upo_ref[...].astype(F32) + up_buf[...].astype(F32)).astype(BF16)
     down_sum[...] = (dno_ref[...].astype(F32) + down_buf[...].astype(F32)).astype(BF16)
-    for copy in second:
-        copy.wait_recv()
-
-    def add_x(i, carry):
-        total = r1[0, i].astype(jnp.float32)
-        if xs == 4:
-            total = total + r2[0, i].astype(jnp.float32) + r2[1, i].astype(jnp.float32)
-        w2[i] = total.astype(jnp.bfloat16)
-        return carry
-
-    lax.fori_loop(0, zs, add_x, 0)
-
-    third = []
-    for d in range(1, ys):
-        src = w2.at[:, pl.ds(pl.multiple_of(y_at(d) * chunk, 16), chunk)]
-        copy = send(src, r3.at[d - 1], s3s.at[d - 1], s3r.at[d - 1], y_peer(d))
-        third.append(copy)
-        pending.append(copy)
-    edges.append(send(up_sum, low_buf, ess.at[3], esr.at[3], after))
-    edges.append(send(down_sum, high_buf, ess.at[4], esr.at[4], before))
-    pending += edges
-    for copy in third:
-        copy.wait_recv()
-
-    def add_y(i, carry):
-        total = w2[i, pl.ds(pl.multiple_of(y * chunk, 16), chunk), :].astype(jnp.float32)
-        for d in range(1, ys):
-            total = total + r3[d - 1, i].astype(jnp.float32)
-        w3[i, 0:chunk, :] = total.astype(jnp.bfloat16)
-        w3[i, chunk:, :] = w2[i, rows:, :]
-        return carry
-
-    lax.fori_loop(0, zs, add_y, 0)
-
-    fourth = []
-    for d in range(1, zs):
-        copy = send(w3.at[z_at(d)], r4.at[d - 1], s4s.at[d - 1], s4r.at[d - 1], z_peer(d))
-        fourth.append(copy)
-        pending.append(copy)
-    for copy in fourth:
-        copy.wait_recv()
-    total = w3[z].astype(jnp.float32)
-    for d in range(1, zs):
-        total = total + r4[d - 1].astype(jnp.float32)
-
-    s5[...] = total[:chunk].astype(jnp.bfloat16)
-    if hs > 1:
-        fifth = send(s5, r5, s5s.at[0], s5r.at[0], h_peer())
-        pending.append(fifth)
-    ts[...] = (total[chunk:] * norm_factor).astype(jnp.bfloat16)
-    first_row = ((core * xs + x) * zs + z) * ts.shape[0]
-    handed = pltpu.make_async_remote_copy(
-        src_ref=ts,
-        dst_ref=tr,
-        send_sem=t8s.at[0],
-        recv_sem=t8r.at[0],
-        device_id=before,
-        device_id_type=MESH,
-    )
-    tf[core, x, z] = ts[...]
 
     @pl.when(first_row < PART_A)
     def _():
         handed.start()
-        handed.wait_recv()
-        row = first_row + lax.broadcasted_iota(jnp.int32, ts.shape, 0)
-        tf[core, x, z] = jnp.where(
-            row < PART_A, tr[...].astype(jnp.float32), ts[...].astype(jnp.float32)
-        ).astype(jnp.bfloat16)
-        handed.wait_send()
-
-    table_z = []
+        handed.wait()
+
+        def choose(i, carry):
+            row = first_row + i * trows + lax.broadcasted_iota(jnp.int32, (trows, 128), 0)
+            tab_sum[i] = jnp.where(
+                row < PART_A, tab_hand[i].astype(F32), tab_sum[i].astype(F32)
+            ).astype(BF16)
+            return carry
+
+        lax.fori_loop(0, zs, choose, 0)
+
+    pending.append(None)
+    table_z = [
+        send(tab_sum.at[at(z, d, zs)], tab_z.at[d - 1], z_peers[d]) for d in range(1, zs)
+    ]
+
+    arrived(gathered_y)
+    terms = [lambda i: core_buf[0, i]]
+    terms += [lambda i, d=d: y_buf[d, i] for d in range({4: 2, 2: 1, 1: 0}[ys])]
+    add_into(y_sum, terms, half)
+    along_x = [
+        send(y_sum.at[pl.ds(at(x, d, xs) * zs, zs)], x_buf.at[d - 1], x_peers[d])
+        for d in range(1, xs)
+    ]
+    edges.append(send(up_sum, low_buf, after))
+    edges.append(send(down_sum, high_buf, before))
+
+    arrived(table_z)
+    total = tab_sum[z].astype(F32)
     for d in range(1, zs):
-        copy = send(
-            tf.at[core, x, z], tf.at[core, x, z], t4s.at[d - 1], t4r.at[d - 1], z_peer(d)
-        )
-        table_z.append(copy)
-        pending.append(copy)
-    share = s5[...].astype(jnp.float32)
+        total = total + tab_z[d - 1].astype(F32)
+    tab_all[core, x, z] = (total * norm_factor).astype(BF16)
+    own = tab_all.at[core, x, z]
+    back_z = [send(own, own, z_peers[d]) for d in range(1, zs)]
+
+    arrived(along_x)
+    terms = [lambda i: y_sum[base + i]]
+    terms += [lambda i, d=d: x_buf[d - 1, i] for d in range(1, xs)]
+    add_into(x_sum, terms, zs)
+    along_z = [send(x_sum.at[at(z, d, zs)], z_buf.at[d - 1], z_peers[d]) for d in range(1, zs)]
+
+    arrived(back_z)
+    own = tab_all.at[core, x]
+    back_x = [send(own, own, x_peers[d]) for d in range(1, xs)]
+
+    arrived(along_z)
+    total = x_sum[z].astype(F32)
+    for d in range(1, zs):
+        total = total + z_buf[d - 1].astype(F32)
     if hs > 1:
-        fifth.wait_recv()
-        share = share + r5[...].astype(jnp.float32)
-    mine = pl.ds(pl.multiple_of(y * chunk, 8), chunk)
-    pf[mine, :] = share * norm_factor
-    sixth = []
-    for d in range(1, ys):
-        copy = send(pf.at[mine], pf.at[mine], s6s.at[d - 1], s6r.at[d - 1], y_peer(d))
-        sixth.append(copy)
-        pending.append(copy)
-    for copy in table_z:
-        copy.wait_recv()
-    table_x = []
-    for d in range(1, xs):
-        copy = send(tf.at[core, x], tf.at[core, x], t6s.at[d - 1], t6r.at[d - 1], x_peer(d))
-        table_x.append(copy)
-        pending.append(copy)
-    for copy in table_x:
-        copy.wait_recv()
-    table_core = send(tf.at[core], tf.at[core], t7s.at[0], t7r.at[0], core_peer())
-    pending.append(table_core)
-    for copy in sixth:
-        copy.wait_recv()
-    p_ref[...] = pf[...]
-    for copy in edges[2:]:
-        copy.wait_recv()
+        h_send[...] = total.astype(BF16)
+        across = send(h_send, h_buf, far)
+    arrived(back_x)
+    own = tab_all.at[core]
+    back_core = send(own, own, other_core)
+    if hs > 1:
+        across.wait_recv()
+        total = h_send[...].astype(F32) + h_buf[...].astype(F32)
+    rows = pl.ds(pl.multiple_of(y * chunk, 8), chunk)
+    share[rows, :] = total * norm_factor
+    back_y = [send(share.at[rows], share.at[rows], y_peers[d]) for d in range(1, ys)]
+    arrived(edges[2:])
     par_out[...] = par_buf[...]
     low_out[...] = low_buf[...]
     high_out[...] = high_buf[...]
-    table_core.wait_recv()
-    t_ref[...] = tf[...]
+    back_core.wait_recv()
+    t_ref[...] = tab_all[...]
+    arrived(back_y)
+    p_ref[...] = share[...]
     for copy in pending:
-        copy.wait_send()
-
-
-def reduce_all(pieces, edges, rows, norm_factor, dims):
+        if copy is not None:
+            copy.wait_send()
+
+
+def reduce_all(pieces, tables, edges, norm_factor, dims):
     cores, xs, zs, ys, hs = dims
-    height = pieces.shape[1]
-    trows = height - rows
-    chunk = rows // ys
-    bf16 = jnp.bfloat16
-    sem = pltpu.SemaphoreType.DMA
-    cut = height // 32 * 16
-    counts = [xs, 6, ys - 1, zs - 1, 1, zs - 1, ys - 1, xs - 1, 1, 1]
-    sems = []
-    for count in counts:
-        sems += [sem((max(count, 1),)), sem((max(count, 1),))]
+    half = xs * zs
+    chunk = pieces.shape[2]
+    trows = tables.shape[1]
+    sem = pltpu.SemaphoreType.DMA((64,))
     vmem = pl.BlockSpec(memory_space=pltpu.VMEM)
+    side = (128, 128)
+    all_tables = (cores, xs, zs, trows, 128)
+    outs = [((ys * chunk, 128), F32), (all_tables, BF16), ((FINE, C_F), BF16)]
+    outs += [(side, BF16), (side, BF16)]
+    buffers = [
+        (FINE, C_F),
+        *[side] * 6,
+        (ys, half, chunk, 128),
+        (half // 2, chunk, 128),
+        (half - half // 2, chunk, 128),
+        (2, half, chunk, 128),
+        (half, chunk, 128),
+        (max(xs - 1, 1), zs, chunk, 128),
+        (zs, chunk, 128),
+        (max(zs - 1, 1), chunk, 128),
+        (chunk, 128),
+        (chunk, 128),
+        None,
+        (half, trows, 128),
+        (max(xs - 1, 1), zs, trows, 128),
+        (zs, trows, 128),
+        (zs, trows, 128),
+        (max(zs - 1, 1), trows, 128),
+        all_tables,
+    ]
+    scratch = [
+        pltpu.VMEM((ys * chunk, 128), F32) if shape is None else pltpu.VMEM(shape, BF16)
+        for shape in buffers
+    ]
     return pl.pallas_call(
-        functools.partial(reduce_body, dims, rows, norm_factor),
-        out_shape=(
-            jax.ShapeDtypeStruct((rows, 128), jnp.float32),
-            jax.ShapeDtypeStruct((cores, xs, zs, trows, 128), bf16),
-            jax.ShapeDtypeStruct((FINE, C_F), bf16),
-            jax.ShapeDtypeStruct((128, 128), bf16),
-            jax.ShapeDtypeStruct((128, 128), bf16),
-        ),
-        in_specs=[vmem] * 6,
+        functools.partial(reduce_body, dims, norm_factor),
+        out_shape=tuple(jax.ShapeDtypeStruct(shape, dtype) for shape, dtype in outs),
+        in_specs=[vmem] * 7,
         out_specs=(vmem,) * 5,
-        scratch_shapes=[pltpu.VMEM((FINE, C_F), bf16)]
-        + [pltpu.VMEM((128, 128), bf16)] * 6
-        + [sem((5,)), sem((5,))]
-        + [pltpu.VMEM((zs, cut, 128), bf16), pltpu.VMEM((zs, height - cut, 128), bf16)]
-        + [
-            pltpu.VMEM((xs, zs, height, 128), bf16),
-            pltpu.VMEM((2, zs, height, 128), bf16),
-            pltpu.VMEM((zs, height, 128), bf16),
-            pltpu.VMEM((max(ys - 1, 1), zs, chunk, 128), bf16),
-            pltpu.VMEM((zs, chunk + trows, 128), bf16),
-            pltpu.VMEM((max(zs - 1, 1), chunk + trows, 128), bf16),
-            pltpu.VMEM((chunk, 128), bf16),
-            pltpu.VMEM((chunk, 128), bf16),
-            pltpu.VMEM((rows, 128), jnp.float32),
-            pltpu.VMEM((cores, xs, zs, trows, 128), bf16),
-            pltpu.VMEM((trows, 128), bf16),
-            pltpu.VMEM((trows, 128), bf16),
-        ]
-        + sems,
+        scratch_shapes=scratch + [sem, sem],
         compiler_params=pltpu.CompilerParams(
             collective_id=7, has_side_effects=True, vmem_limit_bytes=VMEM_BYTES
         ),
-        cost_estimate=lasting(45),
+        cost_estimate=lasting(35),
         name="grad_reduce",
-    )(pieces, *edges)
+    )(pieces, tables, *edges)
 
 
 def shards(
@@ -1288,6 +1244,14 @@
         1,
         "halo",
         10,
+    )
+    bias_a, bias_b, bias_c, bias_q = call(
+        bias_body,
+        [((2, 432, 144), F32), ((2, 240, 160), F32), ((2, 240, 160), F32), ((2, 432, 160), F32)],
+        (fine_rows, table_before.reshape(PART_A, 128), coarse_rows),
+        (),
+        "bias_terms",
+        4,
     )
     (
         hat,
@@ -1338,8 +1302,9 @@
             merge_weight,
             coarse_gain,
             coarse_shift,
-            fine_rows,
-            table_before.reshape(PART_A, 128),
+            bias_a,
+            bias_b,
+            bias_c,
         ),
         (),
         "fine_forward",
@@ -1368,7 +1333,7 @@
             coarse_qkv_bias,
             coarse_proj,
             coarse_proj_bias,
-            coarse_rows,
+            bias_q,
         ),
         [
             pltpu.VMEM((72, C_C), F32),
@@ -1397,7 +1362,7 @@
         core, x_at, z_at = (index % cores, index // cores % xs, index // (cores * xs))
         starts.append(((core * xs + x_at) * zs + z_at, index * segment // 128))
     trows = TABLE_ROWS // lon_count
-    fine_out_grad, own_grad, par_grad, upo_grad, upp_grad, dno_grad, dnp_grad, pieces = call(
+    fine_out_grad, own_grad, *edges, pieces, table_pieces = call(
         functools.partial(fine_back_body, starts, rows),
         [
             ((FINE, C_F), F32),
@@ -1407,7 +1372,8 @@
             side,
             side,
             side,
-            ((lon_count, rows + trows, 128), BF16),
+            ((ys, lon_count, rows // ys, 128), BF16),
+            ((lon_count, trows, 128), BF16),
         ],
         (
             norm_part,
@@ -1444,7 +1410,7 @@
         9,
     )
     owned, table_sum, par_back, low_back, high_back = reduce_all(
-        pieces, (par_grad, upo_grad, upp_grad, dno_grad, dnp_grad), rows, norm_factor, dims
+        pieces, table_pieces, edges, norm_factor, dims
     )
     shift = lax.rem(lon * segment, 128)
     param_grads = lax.dynamic_slice(owned.reshape(-1), (shift,), (segment,))

time: 160 us -> 133 us (0.83)
  the two profiles are of different devices: /device:TPU:29 before, /device:TPU:8 now
where the time goes in v1:
time: 133 us
  Pallas kernels  125 us (94%)
  local copies, waits for them, and re-layouts  7.08 us (5%)
    pallas_call x1, Pallas kernels, reduce_all(): pl.pallas_call(functools.partial(reduce_body, dims, norm_factor), out_sha...  58.7 us
    pallas_call x3, Pallas kernels, exchange_call(): pl.pallas_call(body, out_shape=tuple((jax.ShapeDtypeStruct(shape, dtype)...  37.2 us
    pallas_call x6, Pallas kernels, call(): pl.pallas_call(body, out_shape=tuple((jax.ShapeDtypeStruct(shape, dtype)...  28.7 us

profile of v1, /device:TPU:8, one launch (start us, length us, event | category | flops | bytes accessed | tf_op | source)
XLA Modules:
  0.0 132.7 jit_solution(15811036826557400432)
XLA Ops:
  0.6 1.7 %reshape.31.tf_ref = bf16[576,138]{1,0:T(8,128)(2,1)S(1)} reshape(bf16[2,39744]{1,0:T(2,128)(2,1)} %param.26) | data formatting | bytes 317952 | tf_op jit(solution)/shard_map/reshape | solution.py:1220
  2.4 0.0 copy-start.4
  2.4 0.9 copy-done.4
  3.3 0.8 prepare.1
  4.1 0.0 copy-start.17
  4.1 25.6 %halo.1 = (bf16[304,192]{1,0:T(8,128)(2,1)S(1)}, bf16[128,128]{1,0:T(8,128)(2,1)S(1)}, bf16[128,128]{1,0:T(8,128)(2,1)S(1)}, bf16[128,128]{1,0:T(8,128)(2,1)S(1)...) custom-call(bf16[304,192]{1,0:T(8,128)(2,1)S(1)} %get-tuple-element.55.x_ref.own_ref, ...), custom_call_target="tpu_custom_call" | custom-call | flops 20000000000 | bytes 36900000 | tf_op jit(solution)/shard_map/halo/pallas_call | solution.py:328
  29.7 0.9 reshape.33.tc_ref
  30.6 0.0 copy-start.1
  30.6 0.0 copy-start.3
  30.6 0.0 copy-start.5
  30.6 0.0 copy-start.8
  30.6 0.0 copy-start.9
  30.7 0.0 copy-start.10
  30.7 0.0 copy-start.11
  30.7 0.0 copy-start.13
  30.7 0.0 copy-start.14
  30.7 0.0 copy-start.15
  30.7 0.0 copy-start.16
  30.7 3.3 %bias_terms.1 = (f32[2,432,144]{2,1,0:T(8,128)S(1)}, f32[2,240,160]{2,1,0:T(8,128)S(1)}, f32[2,240,160]{2,1,0:T(8,128)S(1)}, f32[2,432,160]{2,1,0:T(8,128)S(1)}) custom-call(bf16[576,138]{1,0:T(8,128)(2,1)S(1)} %reshape.31.tf_ref, bf16[256,128]{1,0:T(8,128)(2,1)S(1)} %bitcast.19, bf16[576,138]{1,0:T(8,128)(2,1)S(1)} %reshape.33.tc_ref), custom_call_target="tpu_custom_call" | custom-call | flops 8000000000 | bytes 14760000 | tf_op jit(solution)/shard_map/bias_terms/pallas_call | solution.py:245
  34.2 6.6 %fine_forward.1 = (f32[928,192]{1,0:T(8,128)S(1)}, bf16[928,192]{1,0:T(8,128)(2,1)S(1)}, f32[304,192]{1,0:T(8,128)S(1)}, f32[928,192]{1,0:T(8,128)S(1)}, f32[928...) custom-call(bf16[304,192]{1,0:T(8,128)(2,1)S(1)} %get-tuple-element., ...), custom_call_target="tpu_custom_call" | custom-call | flops 20000000000 | bytes 36900000 | tf_op jit(solution)/shard_map/fine_forward/pallas_call | solution.py:245
  40.8 0.0 copy-start
  40.8 0.0 copy-start.6
  40.8 0.0 copy-start.7
  40.8 5.7 %coarse_gather.1.group_ref = bf16[4,80,384]{2,1,0:T(8,128)(2,1)S(1)} custom-call(bf16[80,384]{1,0:T(8,128)(2,1)S(1)} %get-tuple-element.68.own_ref), custom_call_target="tpu_custom_call" | custom-call | flops 10000000000 | bytes 18450000 | tf_op jit(solution)/shard_map/coarse_gather/pallas_call | solution.py:328
  46.6 6.9 %coarse_attention.1 = (bf16[6,3,4,384]{3,2,1,0:T(4,128)(2,1)}, bf16[4,80,384]{2,1,0:T(8,128)(2,1)S(1)}, f32[80,384]{1,0:T(8,128)S(1)}, f32[4620,128]{1,0:T(8,128...) custom-call(bf16[4,80,384]{2,1,0:T(8,128)(2,1)S(1)} %coarse_gather.1.group_ref, ...), custom_call_target="tpu_custom_call" | custom-call | flops 14000000000 | bytes 25830000 | tf_op jit(solution)/shard_map/coarse_attention/pallas_call | solution.py:245
  53.5 5.9 %coarse_scatter.1.part_ref = f32[80,384]{1,0:T(8,128)S(1)} custom-call(bf16[4,80,384]{2,1,0:T(8,128)(2,1)S(1)} %get-tuple-element.72.parts_ref), custom_call_target="tpu_custom_call" | custom-call | flops 10000000000 | bytes 18450000 | tf_op jit(solution)/shard_map/coarse_scatter/pallas_call | solution.py:328
  59.4 8.6 %fine_backward.1 = (f32[304,192]{1,0:T(8,128)S(1)}, f32[304,192]{1,0:T(8,128)S(1)}, bf16[304,192]{1,0:T(8,128)(2,1)S(1)}, bf16[128,128]{1,0:T(8,128)(2,1)S(1)}, ...) custom-call(f32[80,384]{1,0:T(8,128)S(1)} %coarse_scatter.1.part_ref, ...), custom_call_target="tpu_custom_call" | custom-call | flops 17999998976 | bytes 33210000 | tf_op jit(solution)/shard_map/fine_backward/pallas_call | solution.py:245
  68.0 58.7 %grad_reduce.1 = (f32[128,128]{1,0:T(8,128)S(1)}, bf16[2,4,8,32,128]{4,3,2,1,0:T(8,128)(2,1)S(1)}, bf16[304,192]{1,0:T(8,128)(2,1)S(1)}, bf16[128,128]{1,0:T(8,128)(2,1)S(1)}, bf16[128,128]{1,0:T(8,128)(2,1)S(1)}) custom-call(bf16[4,64,32,128]{3,2,1,0:T(8,128)(2,1)S(1)} %get-tuple-element.90.g_ref, bf16[64,32,128]{2,1,0:T(8,128)(2,1)S(1)} %get-tuple-element.91.gt_ref, ...), custom_call_target="tpu_custom_call" | custom-call | flops 70000001024 | bytes 129150000 | tf_op jit(solution)/shard_map/grad_reduce/pallas_call | solution.py:1182
  126.7 2.5 %final.1 = (bf16[12,6,4,192]{3,2,1,0:T(4,128)(2,1)}, f32[576,138]{1,0:T(8,128)S(1)}, f32[576,138]{1,0:T(8,128)S(1)}) custom-call(bf16[304,192]{1,0:T(8,128)(2,1)S(1)} %get-tuple-element.55.x_ref.own_ref, f32[192]{0:T(256)S(1)} %copy-done.16, f32[304,192]{1,0:T(8,128)S(1)} %get-tuple-element.88.fog_ref, f32[304,192]{1,0:T(8,128)S(1)} %get-tuple-element.89.own_ref, ...), custom_call_target="tpu_custom_call" | custom-call | flops 4000000000 | bytes 7380000 | tf_op jit(solution)/shard_map/final/pallas_call | solution.py:245
  129.2 0.7 dynamic_slice.3
  130.0 1.4 %reshape.36 = f32[2,39744]{1,0:T(2,128)} reshape(f32[576,138]{1,0:T(8,128)S(1)} %get-tuple-element.103) | data formatting | bytes 635904 | tf_op jit(solution)/shard_map/reshape | solution.py:1438
  131.3 1.4 %reshape.37 = f32[2,39744]{1,0:T(2,128)} reshape(f32[576,138]{1,0:T(8,128)S(1)} %get-tuple-element.104) | data formatting | bytes 635904 | tf_op jit(solution)/shard_map/reshape | solution.py:1439
  (19 shorter events, 0.0 us)
Async XLA Ops:
  2.4 0.9 copy-start.4
  4.1 25.6 %copy-start.17 = (bf16[2,39744]{1,0:T(2,128)(2,1)S(1)}, bf16[2,39744]{1,0:T(2,128)(2,1)}, u32[]{:S(2)}) copy-start(bf16[2,39744]{1,0:T(2,128)(2,1)} %param.36) | copy-start | bytes 476932
  30.6 3.5 %copy-start.1 = (bf16[768,384]{1,0:T(8,128)(2,1)S(1)}, bf16[768,384]{1,0:T(8,128)(2,1)}, u32[]{:S(2)}) copy-start(bf16[768,384]{1,0:T(8,128)(2,1)} %merge_ref.3) | copy-start | bytes 1769476
  30.6 3.5 %copy-start.3 = (bf16[192,576]{1,0:T(8,128)(2,1)S(1)}, bf16[192,576]{1,0:T(8,128)(2,1)}, u32[]{:S(2)}) copy-start(bf16[192,576]{1,0:T(8,128)(2,1)} %qkv_ref.5) | copy-start | bytes 663556
  30.6 3.5 %copy-start.5 = (bf16[192,192]{1,0:T(8,128)(2,1)S(1)}, bf16[192,192]{1,0:T(8,128)(2,1)}, u32[]{:S(2)}) copy-start(bf16[192,192]{1,0:T(8,128)(2,1)} %proj_ref.5) | copy-start | bytes 221188
  30.6 3.5 %copy-start.8 = (f32[576]{0:T(1024)S(1)}, f32[576]{0:T(1024)}, u32[]{:S(2)}) copy-start(f32[576]{0:T(1024)} %qkv_bias_ref.2) | copy-start | bytes 6916
  30.6 3.5 %copy-start.9 = (f32[768]{0:T(1024)S(1)}, f32[768]{0:T(1024)}, u32[]{:S(2)}) copy-start(f32[768]{0:T(1024)} %merge_shift_ref.1) | copy-start | bytes 9220
  30.7 3.5 %copy-start.10 = (f32[768]{0:T(1024)S(1)}, f32[768]{0:T(1024)}, u32[]{:S(2)}) copy-start(f32[768]{0:T(1024)} %merge_gain_ref.3) | copy-start | bytes 9220
  30.7 3.5 %copy-start.11 = (f32[384]{0:T(512)S(1)}, f32[384]{0:T(512)}, u32[]{:S(2)}) copy-start(f32[384]{0:T(512)} %coarse_shift_ref.1) | copy-start | bytes 4612
  30.7 3.5 %copy-start.13 = (f32[384]{0:T(512)S(1)}, f32[384]{0:T(512)}, u32[]{:S(2)}) copy-start(f32[384]{0:T(512)} %cgain_ref.1) | copy-start | bytes 4612
  30.7 3.5 %copy-start.14 = (f32[192]{0:T(256)S(1)}, f32[192]{0:T(256)}, u32[]{:S(2)}) copy-start(f32[192]{0:T(256)} %shift_ref.1) | copy-start | bytes 2308
  30.7 3.5 %copy-start.15 = (f32[192]{0:T(256)S(1)}, f32[192]{0:T(256)}, u32[]{:S(2)}) copy-start(f32[192]{0:T(256)} %proj_bias_ref.2) | copy-start | bytes 2308
  30.7 3.5 %copy-start.16 = (f32[192]{0:T(256)S(1)}, f32[192]{0:T(256)}, u32[]{:S(2)}) copy-start(f32[192]{0:T(256)} %gain_ref.3) | copy-start | bytes 2308
  40.8 5.8 %copy-start = (bf16[384,1152]{1,0:T(8,128)(2,1)S(1)}, bf16[384,1152]{1,0:T(8,128)(2,1)}, u32[]{:S(2)}) copy-start(bf16[384,1152]{1,0:T(8,128)(2,1)} %qkv_ref.4) | copy-start | bytes 2654212
  40.8 5.8 %copy-start.2 = (bf16[384,384]{1,0:T(8,128)(2,1)S(1)}, bf16[384,384]{1,0:T(8,128)(2,1)}, u32[]{:S(2)}) copy-start(bf16[384,384]{1,0:T(8,128)(2,1)} %proj_ref.4) | copy-start | bytes 884740
  40.8 5.8 %copy-start.6 = (bf16[1,4,6,3,384]{4,1,3,2,0:T(4,128)(2,1)S(1)}, bf16[1,4,6,3,384]{4,1,3,2,0:T(4,128)(2,1)}, u32[]{:S(2)}) copy-start(bf16[1,4,6,3,384]{4,1,3,2,0:T(4,128)(2,1)} %param.37) | copy-start | bytes 165892
  40.8 5.8 %copy-start.7 = (f32[1152]{0:T(1024)S(1)}, f32[1152]{0:T(1024)}, u32[]{:S(2)}) copy-start(f32[1152]{0:T(1024)} %qkv_bias_ref.3) | copy-start | bytes 13828
  40.8 5.8 %copy-start.12 = (f32[384]{0:T(512)S(1)}, f32[384]{0:T(512)}, u32[]{:S(2)}) copy-start(f32[384]{0:T(512)} %proj_bias_ref.3) | copy-start | bytes 4612

commit v2 on v1

--- a/solution.py
+++ b/solution.py
@@ -348,11 +348,11 @@
     others = [lax.rem(rank + d, size) for d in range(1, size)]
     near = [(lat, lon - rank + other) for other in others]
     beside = (lat, partner)
-    meet([beside, (up, lon), (down, lon)] + near)
-    x_copy = start_copy(x_ref, par, ss.at[0], rs.at[0], beside)
+    meet([(up, lon), (down, lon), beside] + near)
     low_copy = start_copy(low_ref, upo, ss.at[1], rs.at[1], (down, lon))
     high_copy = start_copy(high_ref, dno, ss.at[2], rs.at[2], (up, lon))
     table_copy = start_copy(tab_ref.at[rank], tab.at[rank], ss.at[3], rs.at[3], (up, lon))
+    x_copy = start_copy(x_ref, par, ss.at[0], rs.at[0], beside)
     copies = [x_copy, low_copy, high_copy, table_copy]
     low_copy.wait_recv()
     relays = [start_copy(upo, upp, ss.at[4], rs.at[4], beside)]
@@ -946,6 +946,7 @@
     tab_core,
     tab_x,
     tab_sum,
+    tab_own,
     tab_hand,
     tab_z,
     tab_all,
@@ -977,10 +978,9 @@
     far = (at(h, 1, hs) * ys + y, lon)
     before, after = ((at(lat, lats - 1, lats), lon), (at(lat, 1, lats), lon))
     beside = (lat, partner_of(lon, cores * half))
-    peers = [other_core, before, after, beside]
-    peers += list(x_peers.values()) + list(y_peers.values()) + list(z_peers.values())
-    if hs > 1:
-        peers.append(far)
+    peers = [before, after] + ([far] if hs > 1 else [])
+    peers += list(z_peers.values())[::-1] + list(y_peers.values()) + list(x_peers.values())
+    peers += [beside, other_core]
     meet(peers)
     pending = []
 
@@ -1047,40 +1047,16 @@
         add_into(left, [lambda i: left[i], lambda i: tail_buf[i]], half - cut)
         gathered_y.append(send(core_buf.at[3, tail], y_buf.at[1, tail], y_peers[3]))
 
+    arrived(edges[:2])
+    up_sum[...] = (upo_ref[...].astype(F32) + up_buf[...].astype(F32)).astype(BF16)
+    down_sum[...] = (dno_ref[...].astype(F32) + down_buf[...].astype(F32)).astype(BF16)
+    edges.append(send(up_sum, low_buf, after))
+    edges.append(send(down_sum, high_buf, before))
     arrived(table_x)
     base = x * zs
     terms = [lambda i: tab_core[base + i]]
     terms += [lambda i, d=d: tab_x[d - 1, i] for d in range(1, xs)]
     add_into(tab_sum, terms, zs)
-    first_row = (core * xs + x) * zs * trows
-    hand_sem = len(pending)
-    handed = pltpu.make_async_remote_copy(
-        src_ref=tab_sum,
-        dst_ref=tab_hand,
-        send_sem=send_sems.at[hand_sem],
-        recv_sem=recv_sems.at[hand_sem],
-        device_id=before,
-        device_id_type=MESH,
-    )
-    arrived(edges[:2])
-    up_sum[...] = (upo_ref[...].astype(F32) + up_buf[...].astype(F32)).astype(BF16)
-    down_sum[...] = (dno_ref[...].astype(F32) + down_buf[...].astype(F32)).astype(BF16)
-
-    @pl.when(first_row < PART_A)
-    def _():
-        handed.start()
-        handed.wait()
-
-        def choose(i, carry):
-            row = first_row + i * trows + lax.broadcasted_iota(jnp.int32, (trows, 128), 0)
-            tab_sum[i] = jnp.where(
-                row < PART_A, tab_hand[i].astype(F32), tab_sum[i].astype(F32)
-            ).astype(BF16)
-            return carry
-
-        lax.fori_loop(0, zs, choose, 0)
-
-    pending.append(None)
     table_z = [
         send(tab_sum.at[at(z, d, zs)], tab_z.at[d - 1], z_peers[d]) for d in range(1, zs)
     ]
@@ -1093,16 +1069,42 @@
         send(y_sum.at[pl.ds(at(x, d, xs) * zs, zs)], x_buf.at[d - 1], x_peers[d])
         for d in range(1, xs)
     ]
-    edges.append(send(up_sum, low_buf, after))
-    edges.append(send(down_sum, high_buf, before))
 
     arrived(table_z)
     total = tab_sum[z].astype(F32)
     for d in range(1, zs):
         total = total + tab_z[d - 1].astype(F32)
-    tab_all[core, x, z] = (total * norm_factor).astype(BF16)
     own = tab_all.at[core, x, z]
-    back_z = [send(own, own, z_peers[d]) for d in range(1, zs)]
+    tab_own[...] = (total * norm_factor).astype(BF16)
+    tab_all[core, x, z] = tab_own[...]
+    first_row = ((core * xs + x) * zs + z) * trows
+
+    def prepared(src, dst, peer):
+        sem = len(pending)
+        copy = pltpu.make_async_remote_copy(
+            src_ref=src,
+            dst_ref=dst,
+            send_sem=send_sems.at[sem],
+            recv_sem=recv_sems.at[sem],
+            device_id=peer,
+            device_id_type=MESH,
+        )
+        pending.append(copy)
+        return copy
+
+    handed = prepared(tab_own, tab_hand, before)
+    pending.pop()
+    pending.append(None)
+    back_z = [prepared(own, own, z_peers[d]) for d in range(1, zs)]
+
+    @pl.when(first_row < PART_A)
+    def _():
+        handed.start()
+
+    @pl.when(first_row >= PART_A)
+    def _():
+        for copy in back_z:
+            copy.start()
 
     arrived(along_x)
     terms = [lambda i: y_sum[base + i]]
@@ -1110,9 +1112,15 @@
     add_into(x_sum, terms, zs)
     along_z = [send(x_sum.at[at(z, d, zs)], z_buf.at[d - 1], z_peers[d]) for d in range(1, zs)]
 
-    arrived(back_z)
-    own = tab_all.at[core, x]
-    back_x = [send(own, own, x_peers[d]) for d in range(1, xs)]
+    @pl.when(first_row < PART_A)
+    def _():
+        handed.wait()
+        row = first_row + lax.broadcasted_iota(jnp.int32, (trows, 128), 0)
+        tab_all[core, x, z] = jnp.where(
+            row < PART_A, tab_hand[...].astype(F32), tab_own[...].astype(F32)
+        ).astype(BF16)
+        for copy in back_z:
+            copy.start()
 
     arrived(along_z)
     total = x_sum[z].astype(F32)
@@ -1121,23 +1129,26 @@
     if hs > 1:
         h_send[...] = total.astype(BF16)
         across = send(h_send, h_buf, far)
-    arrived(back_x)
-    own = tab_all.at[core]
-    back_core = send(own, own, other_core)
+    arrived(back_z)
+    own = tab_all.at[core, x]
+    back_x = [send(own, own, x_peers[d]) for d in range(1, xs)]
     if hs > 1:
         across.wait_recv()
         total = h_send[...].astype(F32) + h_buf[...].astype(F32)
     rows = pl.ds(pl.multiple_of(y * chunk, 8), chunk)
     share[rows, :] = total * norm_factor
     back_y = [send(share.at[rows], share.at[rows], y_peers[d]) for d in range(1, ys)]
+    arrived(back_x)
+    own = tab_all.at[core]
+    back_core = send(own, own, other_core)
     arrived(edges[2:])
     par_out[...] = par_buf[...]
     low_out[...] = low_buf[...]
     high_out[...] = high_buf[...]
+    arrived(back_y)
+    p_ref[...] = share[...]
     back_core.wait_recv()
     t_ref[...] = tab_all[...]
-    arrived(back_y)
-    p_ref[...] = share[...]
     for copy in pending:
         if copy is not None:
             copy.wait_send()
@@ -1171,7 +1182,8 @@
         (half, trows, 128),
         (max(xs - 1, 1), zs, trows, 128),
         (zs, trows, 128),
-        (zs, trows, 128),
+        (trows, 128),
+        (trows, 128),
         (max(zs - 1, 1), trows, 128),
         all_tables,
     ]

time: 133 us -> 123 us (0.925)
  the two profiles are of different devices: /device:TPU:8 before, /device:TPU:1 now
where the time goes in v2:
time: 123 us; the launch traced here: 122 us
  Pallas kernels  114 us (93%)
  local copies, waits for them, and re-layouts  7.08 us (6%)
    pallas_call x3, Pallas kernels, exchange_call(): pl.pallas_call(body, out_shape=tuple((jax.ShapeDtypeStruct(shape, dtype)...  44.3 us
    pallas_call x1, Pallas kernels, reduce_all(): pl.pallas_call(functools.partial(reduce_body, dims, norm_factor), out_sha...  41.1 us
    pallas_call x6, Pallas kernels, call(): pl.pallas_call(body, out_shape=tuple((jax.ShapeDtypeStruct(shape, dtype)...  28.7 us

profile of v2, /device:TPU:1, one launch (start us, length us, event | category | flops | bytes accessed | tf_op | source)
XLA Modules:
  0.0 122.1 jit_solution(8529968687161555776)
XLA Ops:
  0.6 1.7 %reshape.31.tf_ref = bf16[576,138]{1,0:T(8,128)(2,1)S(1)} reshape(bf16[2,39744]{1,0:T(2,128)(2,1)} %param.26) | data formatting | bytes 317952 | tf_op jit(solution)/shard_map/reshape | solution.py:1232
  2.4 0.0 copy-start.4
  2.4 0.9 copy-done.4
  3.3 0.8 prepare.1
  4.1 0.0 copy-start.17
  4.1 27.8 %halo.1 = (bf16[304,192]{1,0:T(8,128)(2,1)S(1)}, bf16[128,128]{1,0:T(8,128)(2,1)S(1)}, bf16[128,128]{1,0:T(8,128)(2,1)S(1)}, bf16[128,128]{1,0:T(8,128)(2,1)S(1)...) custom-call(bf16[304,192]{1,0:T(8,128)(2,1)S(1)} %get-tuple-element.55.x_ref.own_ref, ...), custom_call_target="tpu_custom_call" | custom-call | flops 20000000000 | bytes 36900000 | tf_op jit(solution)/shard_map/halo/pallas_call | solution.py:328
  32.0 0.9 reshape.33.tc_ref
  32.8 0.0 copy-start.1
  32.8 0.0 copy-start.3
  32.9 0.0 copy-start.5
  32.9 0.0 copy-start.8
  32.9 0.0 copy-start.9
  32.9 0.0 copy-start.10
  32.9 0.0 copy-start.11
  32.9 0.0 copy-start.13
  32.9 0.0 copy-start.14
  32.9 0.0 copy-start.15
  33.0 0.0 copy-start.16
  33.0 3.3 %bias_terms.1 = (f32[2,432,144]{2,1,0:T(8,128)S(1)}, f32[2,240,160]{2,1,0:T(8,128)S(1)}, f32[2,240,160]{2,1,0:T(8,128)S(1)}, f32[2,432,160]{2,1,0:T(8,128)S(1)}) custom-call(bf16[576,138]{1,0:T(8,128)(2,1)S(1)} %reshape.31.tf_ref, bf16[256,128]{1,0:T(8,128)(2,1)S(1)} %bitcast.19, bf16[576,138]{1,0:T(8,128)(2,1)S(1)} %reshape.33.tc_ref), custom_call_target="tpu_custom_call" | custom-call | flops 8000000000 | bytes 14760000 | tf_op jit(solution)/shard_map/bias_terms/pallas_call | solution.py:245
  36.4 6.6 %fine_forward.1 = (f32[928,192]{1,0:T(8,128)S(1)}, bf16[928,192]{1,0:T(8,128)(2,1)S(1)}, f32[304,192]{1,0:T(8,128)S(1)}, f32[928,192]{1,0:T(8,128)S(1)}, f32[928...) custom-call(bf16[304,192]{1,0:T(8,128)(2,1)S(1)} %get-tuple-element., ...), custom_call_target="tpu_custom_call" | custom-call | flops 20000000000 | bytes 36900000 | tf_op jit(solution)/shard_map/fine_forward/pallas_call | solution.py:245
  43.0 0.0 copy-start
  43.0 0.0 copy-start.6
  43.0 0.0 copy-start.7
  43.1 10.6 %coarse_gather.1.group_ref = bf16[4,80,384]{2,1,0:T(8,128)(2,1)S(1)} custom-call(bf16[80,384]{1,0:T(8,128)(2,1)S(1)} %get-tuple-element.68.own_ref), custom_call_target="tpu_custom_call" | custom-call | flops 10000000000 | bytes 18450000 | tf_op jit(solution)/shard_map/coarse_gather/pallas_call | solution.py:328
  53.7 6.9 %coarse_attention.1 = (bf16[6,3,4,384]{3,2,1,0:T(4,128)(2,1)}, bf16[4,80,384]{2,1,0:T(8,128)(2,1)S(1)}, f32[80,384]{1,0:T(8,128)S(1)}, f32[4620,128]{1,0:T(8,128...) custom-call(bf16[4,80,384]{2,1,0:T(8,128)(2,1)S(1)} %coarse_gather.1.group_ref, ...), custom_call_target="tpu_custom_call" | custom-call | flops 14000000000 | bytes 25830000 | tf_op jit(solution)/shard_map/coarse_attention/pallas_call | solution.py:245
  60.6 5.9 %coarse_scatter.1.part_ref = f32[80,384]{1,0:T(8,128)S(1)} custom-call(bf16[4,80,384]{2,1,0:T(8,128)(2,1)S(1)} %get-tuple-element.72.parts_ref), custom_call_target="tpu_custom_call" | custom-call | flops 10000000000 | bytes 18450000 | tf_op jit(solution)/shard_map/coarse_scatter/pallas_call | solution.py:328
  66.5 8.6 %fine_backward.1 = (f32[304,192]{1,0:T(8,128)S(1)}, f32[304,192]{1,0:T(8,128)S(1)}, bf16[304,192]{1,0:T(8,128)(2,1)S(1)}, bf16[128,128]{1,0:T(8,128)(2,1)S(1)}, ...) custom-call(f32[80,384]{1,0:T(8,128)S(1)} %coarse_scatter.1.part_ref, ...), custom_call_target="tpu_custom_call" | custom-call | flops 17999998976 | bytes 33210000 | tf_op jit(solution)/shard_map/fine_backward/pallas_call | solution.py:245
  75.1 41.1 %grad_reduce.1 = (f32[128,128]{1,0:T(8,128)S(1)}, bf16[2,4,8,32,128]{4,3,2,1,0:T(8,128)(2,1)S(1)}, bf16[304,192]{1,0:T(8,128)(2,1)S(1)}, bf16[128,128]{1,0:T(8,128)(2,1)S(1)}, bf16[128,128]{1,0:T(8,128)(2,1)S(1)}) custom-call(bf16[4,64,32,128]{3,2,1,0:T(8,128)(2,1)S(1)} %get-tuple-element.90.g_ref, bf16[64,32,128]{2,1,0:T(8,128)(2,1)S(1)} %get-tuple-element.91.gt_ref, ...), custom_call_target="tpu_custom_call" | custom-call | flops 70000001024 | bytes 129150000 | tf_op jit(solution)/shard_map/grad_reduce/pallas_call | solution.py:1194
  116.2 2.5 %final.1 = (bf16[12,6,4,192]{3,2,1,0:T(4,128)(2,1)}, f32[576,138]{1,0:T(8,128)S(1)}, f32[576,138]{1,0:T(8,128)S(1)}) custom-call(bf16[304,192]{1,0:T(8,128)(2,1)S(1)} %get-tuple-element.55.x_ref.own_ref, f32[192]{0:T(256)S(1)} %copy-done.16, f32[304,192]{1,0:T(8,128)S(1)} %get-tuple-element.88.fog_ref, f32[304,192]{1,0:T(8,128)S(1)} %get-tuple-element.89.own_ref, ...), custom_call_target="tpu_custom_call" | custom-call | flops 4000000000 | bytes 7380000 | tf_op jit(solution)/shard_map/final/pallas_call | solution.py:245
  118.7 0.7 dynamic_slice.3
  119.4 1.4 %reshape.36 = f32[2,39744]{1,0:T(2,128)} reshape(f32[576,138]{1,0:T(8,128)S(1)} %get-tuple-element.103) | data formatting | bytes 635904 | tf_op jit(solution)/shard_map/reshape | solution.py:1450
  120.8 1.4 %reshape.37 = f32[2,39744]{1,0:T(2,128)} reshape(f32[576,138]{1,0:T(8,128)S(1)} %get-tuple-element.104) | data formatting | bytes 635904 | tf_op jit(solution)/shard_map/reshape | solution.py:1451
  (19 shorter events, 0.0 us)
Async XLA Ops:
  2.4 0.9 copy-start.4
  4.1 27.9 %copy-start.17 = (bf16[2,39744]{1,0:T(2,128)(2,1)S(1)}, bf16[2,39744]{1,0:T(2,128)(2,1)}, u32[]{:S(2)}) copy-start(bf16[2,39744]{1,0:T(2,128)(2,1)} %param.36) | copy-start | bytes 476932
  32.8 3.5 %copy-start.1 = (bf16[768,384]{1,0:T(8,128)(2,1)S(1)}, bf16[768,384]{1,0:T(8,128)(2,1)}, u32[]{:S(2)}) copy-start(bf16[768,384]{1,0:T(8,128)(2,1)} %merge_ref.3) | copy-start | bytes 1769476
  32.8 3.5 %copy-start.3 = (bf16[192,576]{1,0:T(8,128)(2,1)S(1)}, bf16[192,576]{1,0:T(8,128)(2,1)}, u32[]{:S(2)}) copy-start(bf16[192,576]{1,0:T(8,128)(2,1)} %qkv_ref.5) | copy-start | bytes 663556
  32.9 3.5 %copy-start.5 = (bf16[192,192]{1,0:T(8,128)(2,1)S(1)}, bf16[192,192]{1,0:T(8,128)(2,1)}, u32[]{:S(2)}) copy-start(bf16[192,192]{1,0:T(8,128)(2,1)} %proj_ref.5) | copy-start | bytes 221188
  32.9 3.5 %copy-start.8 = (f32[576]{0:T(1024)S(1)}, f32[576]{0:T(1024)}, u32[]{:S(2)}) copy-start(f32[576]{0:T(1024)} %qkv_bias_ref.2) | copy-start | bytes 6916
  32.9 3.5 %copy-start.9 = (f32[768]{0:T(1024)S(1)}, f32[768]{0:T(1024)}, u32[]{:S(2)}) copy-start(f32[768]{0:T(1024)} %merge_shift_ref.1) | copy-start | bytes 9220
  32.9 3.5 %copy-start.10 = (f32[768]{0:T(1024)S(1)}, f32[768]{0:T(1024)}, u32[]{:S(2)}) copy-start(f32[768]{0:T(1024)} %merge_gain_ref.3) | copy-start | bytes 9220
  32.9 3.5 %copy-start.11 = (f32[384]{0:T(512)S(1)}, f32[384]{0:T(512)}, u32[]{:S(2)}) copy-start(f32[384]{0:T(512)} %coarse_shift_ref.1) | copy-start | bytes 4612
  32.9 3.5 %copy-start.13 = (f32[384]{0:T(512)S(1)}, f32[384]{0:T(512)}, u32[]{:S(2)}) copy-start(f32[384]{0:T(512)} %cgain_ref.1) | copy-start | bytes 4612
  32.9 3.5 %copy-start.14 = (f32[192]{0:T(256)S(1)}, f32[192]{0:T(256)}, u32[]{:S(2)}) copy-start(f32[192]{0:T(256)} %shift_ref.1) | copy-start | bytes 2308
  32.9 3.5 %copy-start.15 = (f32[192]{0:T(256)S(1)}, f32[192]{0:T(256)}, u32[]{:S(2)}) copy-start(f32[192]{0:T(256)} %proj_bias_ref.2) | copy-start | bytes 2308
  33.0 3.5 %copy-start.16 = (f32[192]{0:T(256)S(1)}, f32[192]{0:T(256)}, u32[]{:S(2)}) copy-start(f32[192]{0:T(256)} %gain_ref.3) | copy-start | bytes 2308
  43.0 10.7 %copy-start = (bf16[384,1152]{1,0:T(8,128)(2,1)S(1)}, bf16[384,1152]{1,0:T(8,128)(2,1)}, u32[]{:S(2)}) copy-start(bf16[384,1152]{1,0:T(8,128)(2,1)} %qkv_ref.4) | copy-start | bytes 2654212
  43.0 10.7 %copy-start.2 = (bf16[384,384]{1,0:T(8,128)(2,1)S(1)}, bf16[384,384]{1,0:T(8,128)(2,1)}, u32[]{:S(2)}) copy-start(bf16[384,384]{1,0:T(8,128)(2,1)} %proj_ref.4) | copy-start | bytes 884740
  43.0 10.7 %copy-start.6 = (bf16[1,4,6,3,384]{4,1,3,2,0:T(4,128)(2,1)S(1)}, bf16[1,4,6,3,384]{4,1,3,2,0:T(4,128)(2,1)}, u32[]{:S(2)}) copy-start(bf16[1,4,6,3,384]{4,1,3,2,0:T(4,128)(2,1)} %param.37) | copy-start | bytes 165892
  43.0 10.7 %copy-start.7 = (f32[1152]{0:T(1024)S(1)}, f32[1152]{0:T(1024)}, u32[]{:S(2)}) copy-start(f32[1152]{0:T(1024)} %qkv_bias_ref.3) | copy-start | bytes 13828
  43.0 10.7 %copy-start.12 = (f32[384]{0:T(512)S(1)}, f32[384]{0:T(512)}, u32[]{:S(2)}) copy-start(f32[384]{0:T(512)} %proj_bias_ref.3) | copy-start | bytes 4612

commit v3 on v2

--- a/solution.py
+++ b/solution.py
@@ -47,6 +47,10 @@
     return lax.broadcasted_iota(jnp.int32, (1, n), 1).astype(F32)
 
 
+def index_and_other(n, m, flip):
+    return (along_lanes(n), down_rows(m)) if flip else (down_rows(n), along_lanes(m))
+
+
 def match(a, b):
     return jnp.where(a == b, 1.0, 0.0).astype(BF16)
 
@@ -58,8 +62,8 @@
     return jnp.where(row < 3, low, jnp.where(row < 9, mid, top))
 
 
-def fine_order():
-    at = down_rows(FINE)
+def fine_order(flip=False):
+    at, cells = index_and_other(FINE, 288, flip)
     low, top = (at < MID, at >= TOP)
     edge = jnp.where(top, at - TOP, at)
     mid = at - MID
@@ -74,7 +78,7 @@
     )
     col = jnp.where(in_edge, rest(part, 6), rest(mid, 6))
     code = (row * 6 + col) * 4 + rest(2 * zone + zq + 1, 4)
-    return match(jnp.where(in_edge & (part >= 36), -1.0, code), along_lanes(288))
+    return match(jnp.where(in_edge & (part >= 36), -1.0, code), cells)
 
 
 def coarse_place(at):
@@ -82,33 +86,37 @@
     return (whole(at, 40), whole(part, 18), whole(rest(part, 18), 3), rest(part, 3), part < 36)
 
 
-def coarse_order():
-    zone, zq, row, col, valid = coarse_place(down_rows(COARSE))
+def coarse_order(flip=False):
+    at, cells = index_and_other(COARSE, 72, flip)
+    zone, zq, row, col, valid = coarse_place(at)
     code = (row * 3 + col) * 4 + 2 * zone + zq
-    return match(jnp.where(valid, code, -1.0), along_lanes(72))
-
-
-def quartet_order():
-    at = down_rows(4 * COARSE)
+    return match(jnp.where(valid, code, -1.0), cells)
+
+
+def quartet_order(flip=False):
+    at, tokens = index_and_other(4 * COARSE, FINE, flip)
     p = whole(at, COARSE)
     zone, zq, row, col, valid = coarse_place(rest(at, COARSE))
     rolled = rest(2 * zone + zq + 3, 4)
     source = fine_row(
         whole(rolled, 2), rest(rolled, 2), 2 * row + rest(p, 2), 2 * col + whole(p, 2)
     )
-    return match(jnp.where(valid, source, -1.0), along_lanes(FINE))
+    return match(jnp.where(valid, source, -1.0), tokens)
 
 
 def head_rows(heads, lats, cols, tokens, block):
-    at = down_rows(block * cols)
-    part = rest(at, block)
-    h = whole(part, 2 * lats)
-    zq = whole(rest(part, 2 * lats), lats)
-    code = (zq * lats + rest(part, lats)) * cols + whole(at, block)
-    valid = part < heads * 2 * lats
-    head = jnp.where(valid, h, -1.0)
-    mask = match(head, whole(along_lanes(heads * HEAD), HEAD)).astype(F32)
-    return (match(jnp.where(valid, code, -1.0), along_lanes(tokens)), mask, zq)
+    def parts(at):
+        part = rest(at, block)
+        zq = whole(rest(part, 2 * lats), lats)
+        code = (zq * lats + rest(part, lats)) * cols + whole(at, block)
+        valid = part < heads * 2 * lats
+        return (jnp.where(valid, whole(part, 2 * lats), -1.0), zq, jnp.where(valid, code, -1.0))
+
+    rows = block * cols
+    h, zq, code = parts(down_rows(rows))
+    mask = match(h, whole(along_lanes(heads * HEAD), HEAD)).astype(F32)
+    back = match(parts(along_lanes(rows))[2], down_rows(tokens))
+    return ((match(code, along_lanes(tokens)), back), mask, zq)
 
 
 def pair_keys(size, half):
@@ -151,23 +159,24 @@
     )
 
 
-def table_rows(kind, zk):
+def table_rows(kind, zk, flip=False):
     if kind == "q":
-        at = down_rows(288)
+        at, source = index_and_other(288, 576, flip)
         part = rest(at, 144)
         aq = rest(part, 6)
         lead = (whole(aq, 3) * 2 + whole(at, 144)) * HEADS_C + whole(part, 12)
         zq = whole(rest(part, 12), 6)
-        return match(((lead * 2 + zq) * 2 + zk) * 3 + rest(aq, 3), along_lanes(576))
+        return match(((lead * 2 + zq) * 2 + zk) * 3 + rest(aq, 3), source)
     if kind == "a":
-        at, block, lats, first = (down_rows(144), 72, 6, 0)
+        count, block, lats, first = (144, 72, 6, 0)
     else:
-        at, block, lats, first = (down_rows(80), 40, 3, 3 if kind == "c" else 0)
+        count, block, lats, first = (80, 40, 3, 3 if kind == "c" else 0)
+    at, source = index_and_other(count, 288, flip)
     part = rest(at, block)
     lead = whole(at, block) * HEADS_F + whole(part, 2 * lats)
     zq = whole(rest(part, 2 * lats), lats)
     code = ((lead * 2 + zq) * 2 + zk) * 6 + rest(part, lats) + first
-    return match(jnp.where(part < 12 * lats, code, -1.0), along_lanes(288))
+    return match(jnp.where(part < 12 * lats, code, -1.0), source)
 
 
 def dot(a, b):
@@ -211,22 +220,24 @@
 
 
 def attend(queries, keys, values, rows, mask, bias):
-    packed = dot(rows, queries) * mask
+    spread_out, back = rows
+    packed = dot(spread_out, queries) * mask
     scores = dot_nt(packed, keys) * HEAD ** (-0.5) + bias
     weights = jnp.exp(scores - jnp.max(scores, -1, keepdims=True))
     probs = weights / jnp.sum(weights, -1, keepdims=True)
     mixture = dot(probs, values) * mask
-    return (probs, dot_tn(rows, mixture))
+    return (probs, dot(back, mixture))
 
 
 def attend_back(queries, keys, values, rows, mask, probs, mixture_grad, toep, block):
     factor = HEAD ** (-0.5)
-    packed = dot(rows, queries) * mask
-    grad = dot(rows, mixture_grad) * mask
+    spread_out, back = rows
+    packed = dot(spread_out, queries) * mask
+    grad = dot(spread_out, mixture_grad) * mask
     value_grad = dot_tn(probs, grad)
     prob_grad = dot_nt(grad, values)
     score_grad = probs * (prob_grad - jnp.sum(prob_grad * probs, -1, keepdims=True))
-    query_grad = dot_tn(rows, dot(score_grad, keys) * factor * mask)
+    query_grad = dot(back, dot(score_grad, keys) * factor * mask)
     key_grad = dot_tn(score_grad, packed) * factor
     table = None
     for oq, select in enumerate(toep):
@@ -339,8 +350,8 @@
     )(*args)
 
 
-def halo_body(x_ref, low_ref, high_ref, tab_ref, *refs):
-    outs, bufs, (ss, rs, ts, tr) = (refs[:6], refs[6:12], refs[12:])
+def halo_body(x_ref, low_ref, high_ref, tab_ref, tf_ref, tc_ref, *refs):
+    outs, biases, bufs, (ss, rs, ts, tr) = (refs[:5], refs[5:9], refs[9:15], refs[15:])
     par, upo, upp, dno, dnp, tab = bufs
     lat, lon, up, down, partner = ring_positions()
     size = tab.shape[0]
@@ -354,6 +365,10 @@
     table_copy = start_copy(tab_ref.at[rank], tab.at[rank], ss.at[3], rs.at[3], (up, lon))
     x_copy = start_copy(x_ref, par, ss.at[0], rs.at[0], beside)
     copies = [x_copy, low_copy, high_copy, table_copy]
+    kinds = fine_kinds()
+    store_bias("a", spread("a", tf_ref[0:288, :]), kinds["a"], biases[0])
+    store_bias("b", spread("b", tf_ref[288:576, :]), kinds["b"], biases[1])
+    store_bias("q", spread("q", tc_ref[...]), coarse_kind(), biases[3])
     low_copy.wait_recv()
     relays = [start_copy(upo, upp, ss.at[4], rs.at[4], beside)]
     high_copy.wait_recv()
@@ -364,6 +379,9 @@
     x_copy.wait_recv()
     for copy in relays:
         copy.wait_recv()
+    table = jnp.concatenate([tab[place].astype(F32) for place in range(size)], 0)
+    table = jnp.concatenate([table[c * 80 : (c + 1) * 80] for c in range(3)], 1)
+    store_bias("c", table, kinds["c"], biases[2])
     for copy in copies + relays:
         copy.wait_send()
     for out, buf in zip(outs, bufs):
@@ -457,31 +475,26 @@
     return {"a": mid, "b": edge, "c": edge}
 
 
-def bias_body(tf_ref, tp_ref, tc_ref, out_a, out_b, out_c, out_q):
-    tables = {
-        "a": spread("a", tf_ref[0:288, :]),
-        "b": spread("b", tf_ref[288:576, :]),
-        "c": jnp.concatenate([tp_ref[c * 80 : (c + 1) * 80, :].astype(F32) for c in range(3)], 1),
-    }
+def store_bias(name, table, kind, out):
+    _, _, zq, keys, toep, block = kind
     lat = lax.axis_index("lat")
     late = along_lanes(160) >= 80
-    edges = {
+    edge = {
         "a": 0.0,
         "b": jnp.where(late & (lat == lax.axis_size("lat") - 1), NEGATIVE, 0.0),
         "c": jnp.where(jnp.logical_not(late) & (lat == 0), NEGATIVE, 0.0),
-    }
-    kinds = fine_kinds()
-    for name, out in (("a", out_a), ("b", out_b), ("c", out_c)):
-        _, _, zq, keys, toep, block = kinds[name]
-        for zone in range(2):
-            terms = bias_rows(tables[name], toep, zone, block)
-            out[zone] = terms + banned(keys, zq, zone) + edges[name]
-    _, _, zq = head_rows(HEADS_C, 6, 3, 40, 144)
-    cells = group_keys()
-    toep = toeplitz(cells, 3, 3 * lax.rem(lax.axis_index("lon"), 4).astype(F32))
-    table = spread("q", tc_ref[...])
+        "q": 0.0,
+    }[name]
     for zone in range(2):
-        out_q[zone] = bias_rows(table, toep, zone, 144) + banned(cells, zq, 0)
+        terms = bias_rows(table, toep, zone, block)
+        out[zone] = terms + banned(keys, zq, 0 if name == "q" else zone) + edge
+
+
+def coarse_kind():
+    rows, mask, zq = head_rows(HEADS_C, 6, 3, 40, 144)
+    keys = group_keys()
+    toep = toeplitz(keys, 3, 3 * lax.rem(lax.axis_index("lon"), 4).astype(F32))
+    return (rows, mask, zq, keys, toep, 144)
 
 
 def fine_windows(zone):
@@ -622,8 +635,7 @@
     values,
 ):
     fetch_groups(stage, cot_ref)
-    order = coarse_order()
-    cot = dot(order, stage[...])
+    cot = dot(coarse_order(), stage[...])
     cot_out[...] = cot
     bias = vector(qkv_bias_ref)
     wide = [slice(i * C_C, (i + 1) * C_C) for i in range(3)]
@@ -632,8 +644,7 @@
     keys[...] = rounded(dot(group, qkv_ref[:, wide[1]]) + bias[:, wide[1]])
     values[...] = rounded(dot(group, qkv_ref[:, wide[2]]) + bias[:, wide[2]])
     mixture_grad = rounded(dot_nt(cot, proj_ref[...]))
-    rows, mask, _ = head_rows(HEADS_C, 6, 3, 40, 144)
-    toep = toeplitz(group_keys(), 3, 3 * lax.rem(lax.axis_index("lon"), 4).astype(F32))
+    rows, mask, _, _, toep, _ = coarse_kind()
     mixtures, query_grads, grads = ([], [], [])
     for zone in range(2):
         here = slice(zone * 40, (zone + 1) * 40)
@@ -674,7 +685,7 @@
     flat_store(flat_out, 3465, dot_tn(mixture, cot))
     flat_store(flat_out, 4617, column_sum(cot))
     attn = rounded(dot(mixture, proj_ref[...]) + vector(proj_bias_ref))
-    stage[...] = dot_tn(order, coarse_ref[...] + attn)
+    stage[...] = dot(coarse_order(True), coarse_ref[...] + attn)
     store_groups(out_ref, stage)
 
 
@@ -753,8 +764,7 @@
     flat_store(flat, 3477, column_sum(norm_grad * hat))
     flat_store(flat, 3480, column_sum(norm_grad))
     coarse_grad = rounded(cot_ref[...] + norm_back(hat, scale, norm_grad, vector(cgain_ref)))
-    quartet_sel = quartet_order()
-    quartet = dot(quartet_sel, fine_ref[...])
+    quartet = dot(quartet_order(), fine_ref[...])
     hats, scale = quartet_norm([quartet[p * COARSE : (p + 1) * COARSE] for p in range(4)])
     inners, gains, shifts = ([], [], [])
     merge_gain = vector(merge_gain_ref)
@@ -772,8 +782,9 @@
     second = sum(jnp.sum(i * h, -1, keepdims=True) for i, h in zip(inners, hats)) / width
     grads = jnp.concatenate([scale * (i - first - h * second) for i, h in zip(inners, hats)], 0)
     high = rounded(grads)
-    attn_grad = dot_tn(quartet_sel, high)
-    fog_out[...] = attn_grad + dot_tn(quartet_sel, grads - high)
+    unmerge = quartet_order(True)
+    attn_grad = dot(unmerge, high)
+    fog_out[...] = attn_grad + dot(unmerge, grads - high)
     mixture_grad = rounded(dot_nt(attn_grad, proj_ref[...]))
     weight = dot_tn(mix_ref[...], attn_grad)
     corner = weight[0:1]
@@ -877,7 +888,7 @@
     grad[TOP : TOP + SIDE, :] += unpacked_side(high_ref[...].astype(F32))
     hat, scale = norm_parts(x_ref[...].astype(F32))
     total = fog_ref[...] + norm_back(hat, scale, rounded(grad[...]), vector(gain_ref))
-    stage[...] = dot_tn(fine_order(), total)
+    stage[...] = dot(fine_order(True), total)
     store_groups(token_out, stage)
 
     def part(start, height):
@@ -888,7 +899,7 @@
     def natural(kind, block):
         total = None
         for zk in range(2):
-            term = dot_tn(table_rows(kind, zk), dot_nt(block, table_lanes(zk)))
+            term = dot(table_rows(kind, zk, True), dot_nt(block, table_lanes(zk)))
             total = term if total is None else total + term
         return total
 
@@ -1247,23 +1258,16 @@
         2,
     )
     halo = [own, side, side, side, side, table_part]
-    par, upo, upp, dno, dnp, table_before = exchange_call(
+    bias_a, bias_b = (((2, 432, 144), F32), ((2, 240, 160), F32))
+    par, upo, upp, dno, dnp, bias_a, bias_b, bias_c, bias_q = exchange_call(
         halo_body,
-        halo,
-        (x, low, high, table_send),
+        halo[:5] + [bias_a, bias_b, bias_b, ((2, 432, 160), F32)],
+        (x, low, high, table_send, fine_rows, coarse_rows),
         [pltpu.VMEM(*s) for s in halo],
         (6, max(group - 1, 1)),
         1,
         "halo",
-        10,
-    )
-    bias_a, bias_b, bias_c, bias_q = call(
-        bias_body,
-        [((2, 432, 144), F32), ((2, 240, 160), F32), ((2, 240, 160), F32), ((2, 432, 160), F32)],
-        (fine_rows, table_before.reshape(PART_A, 128), coarse_rows),
-        (),
-        "bias_terms",
-        4,
+        12,
     )
     (
         hat,

time: 123 us -> 120 us (0.976)
  Pallas kernels: 114 us -> 111 us
    pallas_call x6 -> x5, Pallas kernels: 28.7 us -> 25 us  [call(): pl.pallas_call(body, out_shape=tuple((jax.ShapeDtypeStruct(shape, dtype)...]
where the time goes in v3:
time: 120 us; the launch traced here: 119 us
  Pallas kernels  111 us (92%)
  local copies, waits for them, and re-layouts  7.16 us (6%)
    pallas_call x3, Pallas kernels, exchange_call(): pl.pallas_call(body, out_shape=tuple((jax.ShapeDtypeStruct(shape, dtype)...  44.9 us
    pallas_call x1, Pallas kernels, reduce_all(): pl.pallas_call(functools.partial(reduce_body, dims, norm_factor), out_sha...  41.1 us
    pallas_call x5, Pallas kernels, call(): pl.pallas_call(body, out_shape=tuple((jax.ShapeDtypeStruct(shape, dtype)...  25 us

profile of v3, /device:TPU:1, one launch (start us, length us, event | category | flops | bytes accessed | tf_op | source)
XLA Modules:
  0.0 119.2 jit_solution(15613041994925641205)
XLA Ops:
  0.6 1.7 %reshape.28.tf_ref = bf16[576,138]{1,0:T(8,128)(2,1)S(1)} reshape(bf16[2,39744]{1,0:T(2,128)(2,1)} %param.26) | data formatting | bytes 317952 | tf_op jit(solution)/shard_map/reshape | solution.py:1243
  2.4 0.0 copy-start.4
  2.4 0.9 copy-done.4
  3.3 0.8 prepare.1
  4.1 0.1 copy-done.17
  4.2 0.9 reshape.29.tc_ref
  5.1 0.0 copy-start.1
  5.1 0.0 copy-start.3
  5.1 0.0 copy-start.5
  5.1 0.0 copy-start.8
  5.1 0.0 copy-start.9
  5.1 0.0 copy-start.10
  5.2 0.0 copy-start.11
  5.2 0.0 copy-start.13
  5.2 0.0 copy-start.14
  5.2 0.0 copy-start.15
  5.2 0.0 copy-start.16
  5.2 28.4 %halo.1 = (bf16[304,192]{1,0:T(8,128)(2,1)S(1)}, bf16[128,128]{1,0:T(8,128)(2,1)S(1)}, bf16[128,128]{1,0:T(8,128)(2,1)S(1)}, bf16[128,128]{1,0:T(8,128)(2,1)S(1)...) custom-call(bf16[304,192]{1,0:T(8,128)(2,1)S(1)} %get-tuple-element., ...), custom_call_target="tpu_custom_call" | custom-call | flops 24000000000 | bytes 44280000 | tf_op jit(solution)/shard_map/halo/pallas_call | solution.py:339
  33.7 6.6 %fine_forward.1 = (f32[928,192]{1,0:T(8,128)S(1)}, bf16[928,192]{1,0:T(8,128)(2,1)S(1)}, f32[304,192]{1,0:T(8,128)S(1)}, f32[928,192]{1,0:T(8,128)S(1)}, f32[928...) custom-call(bf16[304,192]{1,0:T(8,128)(2,1)S(1)} %get-tuple-element., ...), custom_call_target="tpu_custom_call" | custom-call | flops 20000000000 | bytes 36900000 | tf_op jit(solution)/shard_map/fine_forward/pallas_call | solution.py:256
  40.3 0.0 copy-start
  40.3 0.0 copy-start.2
  40.3 0.0 copy-start.6
  40.3 0.0 copy-start.7
  40.3 10.6 %coarse_gather.1.group_ref = bf16[4,80,384]{2,1,0:T(8,128)(2,1)S(1)} custom-call(bf16[80,384]{1,0:T(8,128)(2,1)S(1)} %get-tuple-element.66.own_ref), custom_call_target="tpu_custom_call" | custom-call | flops 10000000000 | bytes 18450000 | tf_op jit(solution)/shard_map/coarse_gather/pallas_call | solution.py:339
  51.0 6.9 %coarse_attention.1 = (bf16[6,3,4,384]{3,2,1,0:T(4,128)(2,1)}, bf16[4,80,384]{2,1,0:T(8,128)(2,1)S(1)}, f32[80,384]{1,0:T(8,128)S(1)}, f32[4620,128]{1,0:T(8,128...) custom-call(bf16[4,80,384]{2,1,0:T(8,128)(2,1)S(1)} %coarse_gather.1.group_ref, ...), custom_call_target="tpu_custom_call" | custom-call | flops 14000000000 | bytes 25830000 | tf_op jit(solution)/shard_map/coarse_attention/pallas_call | solution.py:256
  57.9 5.9 %coarse_scatter.1.part_ref = f32[80,384]{1,0:T(8,128)S(1)} custom-call(bf16[4,80,384]{2,1,0:T(8,128)(2,1)S(1)} %get-tuple-element.70.parts_ref), custom_call_target="tpu_custom_call" | custom-call | flops 10000000000 | bytes 18450000 | tf_op jit(solution)/shard_map/coarse_scatter/pallas_call | solution.py:339
  63.8 8.6 %fine_backward.1 = (f32[304,192]{1,0:T(8,128)S(1)}, f32[304,192]{1,0:T(8,128)S(1)}, bf16[304,192]{1,0:T(8,128)(2,1)S(1)}, bf16[128,128]{1,0:T(8,128)(2,1)S(1)}, ...) custom-call(f32[80,384]{1,0:T(8,128)S(1)} %coarse_scatter.1.part_ref, ...), custom_call_target="tpu_custom_call" | custom-call | flops 17999998976 | bytes 33210000 | tf_op jit(solution)/shard_map/fine_backward/pallas_call | solution.py:256
  72.4 41.1 %grad_reduce.1 = (f32[128,128]{1,0:T(8,128)S(1)}, bf16[2,4,8,32,128]{4,3,2,1,0:T(8,128)(2,1)S(1)}, bf16[304,192]{1,0:T(8,128)(2,1)S(1)}, bf16[128,128]{1,0:T(8,128)(2,1)S(1)}, bf16[128,128]{1,0:T(8,128)(2,1)S(1)}) custom-call(bf16[4,64,32,128]{3,2,1,0:T(8,128)(2,1)S(1)} %get-tuple-element.88.g_ref, bf16[64,32,128]{2,1,0:T(8,128)(2,1)S(1)} %get-tuple-element.89.gt_ref, ...), custom_call_target="tpu_custom_call" | custom-call | flops 70000001024 | bytes 129150000 | tf_op jit(solution)/shard_map/grad_reduce/pallas_call | solution.py:1205
  113.5 2.1 %final.1 = (bf16[12,6,4,192]{3,2,1,0:T(4,128)(2,1)}, f32[576,138]{1,0:T(8,128)S(1)}, f32[576,138]{1,0:T(8,128)S(1)}) custom-call(bf16[304,192]{1,0:T(8,128)(2,1)S(1)} %get-tuple-element.54.x_ref.own_ref, f32[192]{0:T(256)S(1)} %copy-done.16, f32[304,192]{1,0:T(8,128)S(1)} %get-tuple-element.86.fog_ref, f32[304,192]{1,0:T(8,128)S(1)} %get-tuple-element.87.own_ref, ...), custom_call_target="tpu_custom_call" | custom-call | flops 4000000000 | bytes 7380000 | tf_op jit(solution)/shard_map/final/pallas_call | solution.py:256
  115.7 0.7 dynamic_slice.3
  116.4 1.4 %reshape.32 = f32[2,39744]{1,0:T(2,128)} reshape(f32[576,138]{1,0:T(8,128)S(1)} %get-tuple-element.101) | data formatting | bytes 635904 | tf_op jit(solution)/shard_map/reshape | solution.py:1454
  117.8 1.4 %reshape.33 = f32[2,39744]{1,0:T(2,128)} reshape(f32[576,138]{1,0:T(8,128)S(1)} %get-tuple-element.102) | data formatting | bytes 635904 | tf_op jit(solution)/shard_map/reshape | solution.py:1455
  (18 shorter events, 0.0 us)
Async XLA Ops:
  2.4 0.9 copy-start.4
  3.3 0.9 copy-start.17
  5.1 28.5 %copy-start.1 = (bf16[768,384]{1,0:T(8,128)(2,1)S(1)}, bf16[768,384]{1,0:T(8,128)(2,1)}, u32[]{:S(2)}) copy-start(bf16[768,384]{1,0:T(8,128)(2,1)} %merge_ref.3) | copy-start | bytes 1769476
  5.1 28.5 %copy-start.3 = (bf16[192,576]{1,0:T(8,128)(2,1)S(1)}, bf16[192,576]{1,0:T(8,128)(2,1)}, u32[]{:S(2)}) copy-start(bf16[192,576]{1,0:T(8,128)(2,1)} %qkv_ref.5) | copy-start | bytes 663556
  5.1 28.5 %copy-start.5 = (bf16[192,192]{1,0:T(8,128)(2,1)S(1)}, bf16[192,192]{1,0:T(8,128)(2,1)}, u32[]{:S(2)}) copy-start(bf16[192,192]{1,0:T(8,128)(2,1)} %proj_ref.5) | copy-start | bytes 221188
  5.1 28.5 %copy-start.8 = (f32[576]{0:T(1024)S(1)}, f32[576]{0:T(1024)}, u32[]{:S(2)}) copy-start(f32[576]{0:T(1024)} %qkv_bias_ref.2) | copy-start | bytes 6916
  5.1 28.5 %copy-start.9 = (f32[768]{0:T(1024)S(1)}, f32[768]{0:T(1024)}, u32[]{:S(2)}) copy-start(f32[768]{0:T(1024)} %merge_shift_ref.1) | copy-start | bytes 9220
  5.1 28.5 %copy-start.10 = (f32[768]{0:T(1024)S(1)}, f32[768]{0:T(1024)}, u32[]{:S(2)}) copy-start(f32[768]{0:T(1024)} %merge_gain_ref.3) | copy-start | bytes 9220
  5.2 28.5 %copy-start.11 = (f32[384]{0:T(512)S(1)}, f32[384]{0:T(512)}, u32[]{:S(2)}) copy-start(f32[384]{0:T(512)} %coarse_shift_ref.1) | copy-start | bytes 4612
  5.2 28.5 %copy-start.13 = (f32[384]{0:T(512)S(1)}, f32[384]{0:T(512)}, u32[]{:S(2)}) copy-start(f32[384]{0:T(512)} %cgain_ref.1) | copy-start | bytes 4612
  5.2 28.5 %copy-start.14 = (f32[192]{0:T(256)S(1)}, f32[192]{0:T(256)}, u32[]{:S(2)}) copy-start(f32[192]{0:T(256)} %shift_ref.1) | copy-start | bytes 2308
  5.2 28.5 %copy-start.15 = (f32[192]{0:T(256)S(1)}, f32[192]{0:T(256)}, u32[]{:S(2)}) copy-start(f32[192]{0:T(256)} %proj_bias_ref.2) | copy-start | bytes 2308
  5.2 28.5 %copy-start.16 = (f32[192]{0:T(256)S(1)}, f32[192]{0:T(256)}, u32[]{:S(2)}) copy-start(f32[192]{0:T(256)} %gain_ref.3) | copy-start | bytes 2308
  40.3 10.7 %copy-start = (bf16[384,1152]{1,0:T(8,128)(2,1)S(1)}, bf16[384,1152]{1,0:T(8,128)(2,1)}, u32[]{:S(2)}) copy-start(bf16[384,1152]{1,0:T(8,128)(2,1)} %qkv_ref.4) | copy-start | bytes 2654212
  40.3 10.7 %copy-start.2 = (bf16[384,384]{1,0:T(8,128)(2,1)S(1)}, bf16[384,384]{1,0:T(8,128)(2,1)}, u32[]{:S(2)}) copy-start(bf16[384,384]{1,0:T(8,128)(2,1)} %proj_ref.4) | copy-start | bytes 884740
  40.3 10.7 %copy-start.6 = (bf16[1,4,6,3,384]{4,1,3,2,0:T(4,128)(2,1)S(1)}, bf16[1,4,6,3,384]{4,1,3,2,0:T(4,128)(2,1)}, u32[]{:S(2)}) copy-start(bf16[1,4,6,3,384]{4,1,3,2,0:T(4,128)(2,1)} %param.37) | copy-start | bytes 165892
  40.3 10.7 %copy-start.7 = (f32[1152]{0:T(1024)S(1)}, f32[1152]{0:T(1024)}, u32[]{:S(2)}) copy-start(f32[1152]{0:T(1024)} %qkv_bias_ref.3) | copy-start | bytes 13828
  40.3 10.7 %copy-start.12 = (f32[384]{0:T(512)S(1)}, f32[384]{0:T(512)}, u32[]{:S(2)}) copy-start(f32[384]{0:T(512)} %proj_bias_ref.3) | copy-start | bytes 4612

commit v4 on v3

--- a/solution.py
+++ b/solution.py
@@ -303,11 +303,19 @@
     return (lat, lon, up, down, partner_of(lon, lon_count))
 
 
-def meet(peers):
+def greet(peers):
     barrier = pltpu.get_barrier_semaphore()
     for peer in peers:
         pl.semaphore_signal(barrier, inc=1, device_id=peer, device_id_type=MESH)
-    pl.semaphore_wait(barrier, len(peers))
+
+
+def await_greetings(peers):
+    pl.semaphore_wait(pltpu.get_barrier_semaphore(), len(peers))
+
+
+def meet(peers):
+    greet(peers)
+    await_greetings(peers)
 
 
 def start_copy(src, dst, send_sem, recv_sem, peer):
@@ -333,21 +341,24 @@
         copy.wait_send()
 
 
-def exchange_call(body, outs, args, scratch, counts, collective_id, name, micros):
+def remote_call(body, outs, args, scratch, collective_id, name, micros):
     vmem = pl.BlockSpec(memory_space=pltpu.VMEM)
-    sem = pltpu.SemaphoreType.DMA
     return pl.pallas_call(
         body,
         out_shape=tuple(jax.ShapeDtypeStruct(shape, dtype) for shape, dtype in outs),
         in_specs=[vmem] * len(args),
         out_specs=(vmem,) * len(outs),
-        scratch_shapes=list(scratch) + [sem((count,)) for count in counts for _ in range(2)],
+        scratch_shapes=scratch,
         compiler_params=pltpu.CompilerParams(
             collective_id=collective_id, has_side_effects=True, vmem_limit_bytes=VMEM_BYTES
         ),
         cost_estimate=lasting(micros),
         name=name,
     )(*args)
+
+
+def semaphores(*counts):
+    return [pltpu.SemaphoreType.DMA((count,)) for count in counts for _ in range(2)]
 
 
 def halo_body(x_ref, low_ref, high_ref, tab_ref, tf_ref, tc_ref, *refs):
@@ -388,30 +399,38 @@
         out[...] = buf[...]
 
 
-def group_body(own_ref, out_ref, buf, ss, rs):
+def group_peers():
     lat, lon = (lax.axis_index("lat"), lax.axis_index("lon"))
     place = lax.rem(lon, 4)
     others = [lax.rem(place + d, 4) for d in range(1, 4)]
-    peers = [(lat, lon - place + other) for other in others]
-    meet(peers)
-    buf[place] = own_ref[...]
-    exchange([(own_ref, buf.at[place], peer) for peer in peers], ss, rs)
+    return (place, others, [(lat, lon - place + other) for other in others])
+
+
+def forward_gather_body(*refs):
+    inner, (out_ref, buf, ss, rs) = (refs[:-4], refs[-4:])
+    place, _, peers = group_peers()
+    greet(peers)
+    fine_forward_body(*inner)
+    buf[place] = inner[-1][...]
+    await_greetings(peers)
+    exchange([(buf.at[place], buf.at[place], peer) for peer in peers], ss, rs)
     out_ref[...] = buf[...]
 
 
-def ungroup_body(parts_ref, out_ref, buf, ss, rs):
-    lat, lon = (lax.axis_index("lat"), lax.axis_index("lon"))
-    place = lax.rem(lon, 4)
-    others = [lax.rem(place + d, 4) for d in range(1, 4)]
-    peers = [(lat, lon - place + other) for other in others]
-    meet(peers)
-    exchange(
-        [(parts_ref.at[other], buf.at[d], peers[d]) for d, other in enumerate(others)], ss, rs
-    )
-    total = parts_ref[place].astype(F32)
+def coarse_scatter_body(*refs):
+    inputs, (out_ref, norm_out, own_out, flat_out, table_out, cot_out) = (refs[:9], refs[9:15])
+    stage, keys, values, parts, buf, ss, rs = refs[15:]
+    place, others, peers = group_peers()
+    greet(peers)
+    coarse_body(
+        *inputs, out_ref, parts, own_out, flat_out, table_out, cot_out, stage, keys, values
+    )
+    await_greetings(peers)
+    exchange([(parts.at[other], buf.at[d], peers[d]) for d, other in enumerate(others)], ss, rs)
+    total = parts[place].astype(F32)
     for d in range(3):
         total = total + buf[d].astype(F32)
-    out_ref[...] = total
+    norm_out[...] = total
 
 
 def spread(kind, table):
@@ -924,6 +943,7 @@
 def reduce_body(
     dims,
     norm_factor,
+    compute,
     g_ref,
     gt_ref,
     par_ref,
@@ -992,7 +1012,9 @@
     peers = [before, after] + ([far] if hs > 1 else [])
     peers += list(z_peers.values())[::-1] + list(y_peers.values()) + list(x_peers.values())
     peers += [beside, other_core]
-    meet(peers)
+    greet(peers)
+    compute()
+    await_greetings(peers)
     pending = []
 
     def send(src, dst, peer):
@@ -1165,18 +1187,37 @@
             copy.wait_send()
 
 
-def reduce_all(pieces, tables, edges, norm_factor, dims):
+def backward_reduce_body(dims, norm_factor, starts, rows, count, *refs):
+    inputs, refs = (refs[:count], refs[count:])
+    fog_out, own_out, *outs = refs[:7]
+    refs = refs[7:]
+    inner, refs = (refs[:5], refs[5:])
+    edges, pieces, tables = (refs[:5], refs[5], refs[6])
+
+    def compute():
+        fine_back_body(
+            starts, rows, *inputs, fog_out, own_out, *edges, pieces, tables, *inner
+        )
+
+    reduce_body(dims, norm_factor, compute, pieces, tables, *edges, *outs, *refs[7:])
+
+
+def backward_reduce(args, starts, rows, trows, norm_factor, dims):
     cores, xs, zs, ys, hs = dims
     half = xs * zs
-    chunk = pieces.shape[2]
-    trows = tables.shape[1]
+    chunk = rows // ys
     sem = pltpu.SemaphoreType.DMA((64,))
-    vmem = pl.BlockSpec(memory_space=pltpu.VMEM)
     side = (128, 128)
     all_tables = (cores, xs, zs, trows, 128)
-    outs = [((ys * chunk, 128), F32), (all_tables, BF16), ((FINE, C_F), BF16)]
+    outs = [((FINE, C_F), F32), ((FINE, C_F), F32)]
+    outs += [((ys * chunk, 128), F32), (all_tables, BF16), ((FINE, C_F), BF16)]
     outs += [(side, BF16), (side, BF16)]
+    wide = [(ALL_ROWS, C_F), (ALL_ROWS, C_F), (3488, 128), (TABLE_ROWS, 128), (2, 200, 128)]
     buffers = [
+        (FINE, C_F),
+        *[side] * 4,
+        (ys, len(starts), chunk, 128),
+        (len(starts), trows, 128),
         (FINE, C_F),
         *[side] * 6,
         (ys, half, chunk, 128),
@@ -1198,22 +1239,15 @@
         (max(zs - 1, 1), trows, 128),
         all_tables,
     ]
-    scratch = [
+    scratch = [pltpu.VMEM(shape, F32) for shape in wide]
+    scratch += [
         pltpu.VMEM((ys * chunk, 128), F32) if shape is None else pltpu.VMEM(shape, BF16)
         for shape in buffers
     ]
-    return pl.pallas_call(
-        functools.partial(reduce_body, dims, norm_factor),
-        out_shape=tuple(jax.ShapeDtypeStruct(shape, dtype) for shape, dtype in outs),
-        in_specs=[vmem] * 7,
-        out_specs=(vmem,) * 5,
-        scratch_shapes=scratch + [sem, sem],
-        compiler_params=pltpu.CompilerParams(
-            collective_id=7, has_side_effects=True, vmem_limit_bytes=VMEM_BYTES
-        ),
-        cost_estimate=lasting(35),
-        name="grad_reduce",
-    )(pieces, tables, *edges)
+    body = functools.partial(
+        backward_reduce_body, dims, norm_factor, starts, rows, len(args)
+    )
+    return remote_call(body, outs, args, scratch + [sem, sem], 7, "fine_backward_reduce", 40)
 
 
 def shards(
@@ -1259,12 +1293,11 @@
     )
     halo = [own, side, side, side, side, table_part]
     bias_a, bias_b = (((2, 432, 144), F32), ((2, 240, 160), F32))
-    par, upo, upp, dno, dnp, bias_a, bias_b, bias_c, bias_q = exchange_call(
+    par, upo, upp, dno, dnp, bias_a, bias_b, bias_c, bias_q = remote_call(
         halo_body,
         halo[:5] + [bias_a, bias_b, bias_b, ((2, 432, 160), F32)],
         (x, low, high, table_send, fine_rows, coarse_rows),
-        [pltpu.VMEM(*s) for s in halo],
-        (6, max(group - 1, 1)),
+        [pltpu.VMEM(*s) for s in halo] + semaphores(6, max(group - 1, 1)),
         1,
         "halo",
         12,
@@ -1283,8 +1316,9 @@
         merged,
         coarse,
         cnorm,
-    ) = call(
-        fine_forward_body,
+        gathered_norm,
+    ) = remote_call(
+        forward_gather_body,
         [
             ((ALL_ROWS, C_F), F32),
             ((ALL_ROWS, C_F), BF16),
@@ -1299,6 +1333,7 @@
             ((4, COARSE, C_F), BF16),
             ((COARSE, C_C), F32),
             ((COARSE, C_C), BF16),
+            ((4, COARSE, C_C), BF16),
         ],
         (
             x,
@@ -1322,19 +1357,16 @@
             bias_b,
             bias_c,
         ),
-        (),
-        "fine_forward",
-        10,
-    )
-    gathered_to = [((4, COARSE, C_C), BF16)]
-    (gathered_norm,) = exchange_call(
-        group_body, gathered_to, (cnorm,), [pltpu.VMEM(*gathered_to[0])], (3,), 2, "coarse_gather", 5
-    )
-    coarse_out, parts, own_part, flat_c, table_q, cot = call(
-        coarse_body,
+        [pltpu.VMEM((4, COARSE, C_C), BF16)] + semaphores(3),
+        2,
+        "fine_forward_gather",
+        11,
+    )
+    coarse_out, norm_part, own_part, flat_c, table_q, cot = remote_call(
+        coarse_scatter_body,
         [
             ((6, 3, 4, C_C), BF16),
-            ((4, COARSE, C_C), BF16),
+            ((COARSE, C_C), F32),
             ((COARSE, C_C), F32),
             ((4620, 128), F32),
             ((288, 384), F32),
@@ -1355,19 +1387,13 @@
             pltpu.VMEM((72, C_C), F32),
             pltpu.VMEM((4 * COARSE, C_C), F32),
             pltpu.VMEM((4 * COARSE, C_C), F32),
+            pltpu.VMEM((4, COARSE, C_C), BF16),
+            pltpu.VMEM((3, COARSE, C_C), BF16),
+            *semaphores(3),
         ],
-        "coarse_attention",
-        7,
-    )
-    (norm_part,) = exchange_call(
-        ungroup_body,
-        [((COARSE, C_C), F32)],
-        (parts,),
-        [pltpu.VMEM((3, COARSE, C_C), BF16)],
-        (3,),
         3,
-        "coarse_scatter",
-        5,
+        "coarse_attention_scatter",
+        12,
     )
     dims = mesh_parts(lat_count, lon_count)
     cores, xs, zs, ys, hs = dims
@@ -1377,20 +1403,7 @@
     for index in range(lon_count):
         core, x_at, z_at = (index % cores, index // cores % xs, index // (cores * xs))
         starts.append(((core * xs + x_at) * zs + z_at, index * segment // 128))
-    trows = TABLE_ROWS // lon_count
-    fine_out_grad, own_grad, *edges, pieces, table_pieces = call(
-        functools.partial(fine_back_body, starts, rows),
-        [
-            ((FINE, C_F), F32),
-            ((FINE, C_F), F32),
-            own,
-            side,
-            side,
-            side,
-            side,
-            ((ys, lon_count, rows // ys, 128), BF16),
-            ((lon_count, trows, 128), BF16),
-        ],
+    fine_out_grad, own_grad, owned, table_sum, par_back, low_back, high_back = backward_reduce(
         (
             norm_part,
             own_part,
@@ -1415,18 +1428,11 @@
             flat_c,
             table_q,
         ),
-        [
-            pltpu.VMEM((ALL_ROWS, C_F), F32),
-            pltpu.VMEM((ALL_ROWS, C_F), F32),
-            pltpu.VMEM((3488, 128), F32),
-            pltpu.VMEM((TABLE_ROWS, 128), F32),
-            pltpu.VMEM((2, 200, 128), F32),
-        ],
-        "fine_backward",
-        9,
-    )
-    owned, table_sum, par_back, low_back, high_back = reduce_all(
-        pieces, table_pieces, edges, norm_factor, dims
+        starts,
+        rows,
+        TABLE_ROWS // lon_count,
+        norm_factor,
+        dims,
     )
     shift = lax.rem(lon * segment, 128)
     param_grads = lax.dynamic_slice(owned.reshape(-1), (shift,), (segment,))

time: 120 us -> 112 us (0.933)
  Pallas kernels: 111 us -> 103 us
    pallas_call x5 -> x2, Pallas kernels: 25 us -> 2.95 us  [call(): pl.pallas_call(body, out_shape=tuple((jax.ShapeDtypeStruct(shape, dtype)...]
    pallas_call x4, Pallas kernels: 86 us -> 99.9 us  [remote_call(): pl.pallas_call(body, out_shape=tuple((jax.ShapeDtypeStruct(shape, dtype)...]
where the time goes in v4:
time: 112 us
  Pallas kernels  103 us (92%)
  local copies, waits for them, and re-layouts  7.79 us (7%)
    pallas_call x4, Pallas kernels, remote_call(): pl.pallas_call(body, out_shape=tuple((jax.ShapeDtypeStruct(shape, dtype)...  99.9 us
    pallas_call x2, Pallas kernels, call(): pl.pallas_call(body, out_shape=tuple((jax.ShapeDtypeStruct(shape, dtype)...  2.95 us

profile of v4, /device:TPU:1, one launch (start us, length us, event | category | flops | bytes accessed | tf_op | source)
XLA Modules:
  0.0 111.6 jit_solution(14916018889945791433)
XLA Ops:
  0.6 1.7 %reshape.28.tf_ref = bf16[576,138]{1,0:T(8,128)(2,1)S(1)} reshape(bf16[2,39744]{1,0:T(2,128)(2,1)} %param.26) | data formatting | bytes 317952 | tf_op jit(solution)/shard_map/reshape | solution.py:1277
  2.4 0.0 copy-start.4
  2.4 0.9 copy-done.4
  3.3 0.8 prepare.1
  4.1 0.1 copy-done.17
  4.2 0.9 reshape.29.tc_ref
  5.1 0.0 copy-start.1
  5.1 0.0 copy-start.3
  5.1 0.0 copy-start.5
  5.1 0.0 copy-start.8
  5.1 0.0 copy-start.9
  5.1 0.0 copy-start.10
  5.2 0.0 copy-start.11
  5.2 0.0 copy-start.13
  5.2 0.0 copy-start.14
  5.2 0.0 copy-start.15
  5.2 0.0 copy-start.16
  5.2 28.4 %halo.1 = (bf16[304,192]{1,0:T(8,128)(2,1)S(1)}, bf16[128,128]{1,0:T(8,128)(2,1)S(1)}, bf16[128,128]{1,0:T(8,128)(2,1)S(1)}, bf16[128,128]{1,0:T(8,128)(2,1)S(1)...) custom-call(bf16[304,192]{1,0:T(8,128)(2,1)S(1)} %get-tuple-element., ...), custom_call_target="tpu_custom_call" | custom-call | flops 24000000000 | bytes 44280000 | tf_op jit(solution)/shard_map/halo/pallas_call | solution.py:346
  33.6 0.0 copy-done.1
  33.7 0.0 copy-start
  33.7 0.0 copy-start.2
  33.7 0.0 copy-start.6
  33.7 0.0 copy-start.7
  33.7 0.0 copy-start.12
  33.8 13.4 %fine_forward_gather.1 = (f32[928,192]{1,0:T(8,128)S(1)}, bf16[928,192]{1,0:T(8,128)(2,1)S(1)}, f32[304,192]{1,0:T(8,128)S(1)}, f32[928,192]{1,0:T(8,128)S(1)}, ...) custom-call(bf16[304,192]{1,0:T(8,128)(2,1)S(1)} %get-tuple-element., ...), custom_call_target="tpu_custom_call" | custom-call | flops 22000001024 | bytes 40590000 | tf_op jit(solution)/shard_map/fine_forward_gather/pallas_call | solution.py:346
  47.3 13.4 %coarse_attention_scatter.1 = (bf16[6,3,4,384]{3,2,1,0:T(4,128)(2,1)S(1)}, f32[80,384]{1,0:T(8,128)S(1)}, f32[80,384]{1,0:T(8,128)S(1)}, f32[4620,128]{1,0:T(8,1...) custom-call(bf16[4,80,384]{2,1,0:T(8,128)(2,1)S(1)} %get-tuple-element.60.refs_0_, ...), custom_call_target="tpu_custom_call" | custom-call | flops 24000000000 | bytes 44280000 | tf_op jit(solution)/shard_map/coarse_attention_scatter/pallas_call | solution.py:346
  60.7 44.6 %fine_backward_reduce.1 = (f32[304,192]{1,0:T(8,128)S(1)}, f32[304,192]{1,0:T(8,128)S(1)}, f32[128,128]{1,0:T(8,128)S(1)}, bf16[2,4,8,32,128]{4,3,2,1,0:T(8,128)...) custom-call(f32[80,384]{1,0:T(8,128)S(1)} %get-tuple-element.65.refs_0_, ...), custom_call_target="tpu_custom_call" | custom-call | flops 80000000000 | bytes 147600000 | tf_op jit(solution)/shard_map/fine_backward_reduce/pallas_call | solution.py:346
  105.3 2.1 %final.1 = (bf16[12,6,4,192]{3,2,1,0:T(4,128)(2,1)}, f32[576,138]{1,0:T(8,128)S(1)}, f32[576,138]{1,0:T(8,128)S(1)}) custom-call(bf16[304,192]{1,0:T(8,128)(2,1)S(1)} %get-tuple-element.48.x_ref.refs_0_, f32[192]{0:T(256)S(1)} %copy-done.16, f32[304,192]{1,0:T(8,128)S(1)} %get-tuple-element.81.fog_ref, f32[304,192]{1,0:T(8,128)S(1)} %get-tuple-element.82.own_ref, ...), custom_call_target="tpu_custom_call" | custom-call | flops 4000000000 | bytes 7380000 | tf_op jit(solution)/shard_map/final/pallas_call | solution.py:256
  107.5 0.7 dynamic_slice.3
  108.2 1.4 %reshape.32 = f32[2,39744]{1,0:T(2,128)} reshape(f32[576,138]{1,0:T(8,128)S(1)} %get-tuple-element.89) | data formatting | bytes 635904 | tf_op jit(solution)/shard_map/reshape | solution.py:1460
  109.6 1.4 %reshape.33 = f32[2,39744]{1,0:T(2,128)} reshape(f32[576,138]{1,0:T(8,128)S(1)} %get-tuple-element.90) | data formatting | bytes 635904 | tf_op jit(solution)/shard_map/reshape | solution.py:1461
  110.9 0.6 copy.25
  (16 shorter events, 0.0 us)
Async XLA Ops:
  2.4 0.9 copy-start.4
  3.3 0.9 copy-start.17
  5.1 28.5 %copy-start.1 = (bf16[768,384]{1,0:T(8,128)(2,1)S(1)}, bf16[768,384]{1,0:T(8,128)(2,1)}, u32[]{:S(2)}) copy-start(bf16[768,384]{1,0:T(8,128)(2,1)} %refs_18_.1) | copy-start | bytes 1769476
  5.1 28.5 %copy-start.3 = (bf16[192,576]{1,0:T(8,128)(2,1)S(1)}, bf16[192,576]{1,0:T(8,128)(2,1)}, u32[]{:S(2)}) copy-start(bf16[192,576]{1,0:T(8,128)(2,1)} %refs_15_.3) | copy-start | bytes 663556
  5.1 28.5 %copy-start.5 = (bf16[192,192]{1,0:T(8,128)(2,1)S(1)}, bf16[192,192]{1,0:T(8,128)(2,1)}, u32[]{:S(2)}) copy-start(bf16[192,192]{1,0:T(8,128)(2,1)} %refs_19_.1) | copy-start | bytes 221188
  5.1 28.5 %copy-start.8 = (f32[576]{0:T(1024)S(1)}, f32[576]{0:T(1024)}, u32[]{:S(2)}) copy-start(f32[576]{0:T(1024)} %refs_9_.1) | copy-start | bytes 6916
  5.1 28.5 %copy-start.9 = (f32[768]{0:T(1024)S(1)}, f32[768]{0:T(1024)}, u32[]{:S(2)}) copy-start(f32[768]{0:T(1024)} %refs_13_.1) | copy-start | bytes 9220
  5.1 28.5 %copy-start.10 = (f32[768]{0:T(1024)S(1)}, f32[768]{0:T(1024)}, u32[]{:S(2)}) copy-start(f32[768]{0:T(1024)} %refs_17_.1) | copy-start | bytes 9220
  5.2 28.5 %copy-start.11 = (f32[384]{0:T(512)S(1)}, f32[384]{0:T(512)}, u32[]{:S(2)}) copy-start(f32[384]{0:T(512)} %refs_16_.2) | copy-start | bytes 4612
  5.2 28.5 %copy-start.13 = (f32[384]{0:T(512)S(1)}, f32[384]{0:T(512)}, u32[]{:S(2)}) copy-start(f32[384]{0:T(512)} %refs_16_.3) | copy-start | bytes 4612
  5.2 28.5 %copy-start.14 = (f32[192]{0:T(256)S(1)}, f32[192]{0:T(256)}, u32[]{:S(2)}) copy-start(f32[192]{0:T(256)} %refs_7_.2) | copy-start | bytes 2308
  5.2 28.5 %copy-start.15 = (f32[192]{0:T(256)S(1)}, f32[192]{0:T(256)}, u32[]{:S(2)}) copy-start(f32[192]{0:T(256)} %refs_11_.1) | copy-start | bytes 2308
  5.2 28.5 %copy-start.16 = (f32[192]{0:T(256)S(1)}, f32[192]{0:T(256)}, u32[]{:S(2)}) copy-start(f32[192]{0:T(256)} %gain_ref.1) | copy-start | bytes 2308
  33.7 13.5 %copy-start = (bf16[384,1152]{1,0:T(8,128)(2,1)S(1)}, bf16[384,1152]{1,0:T(8,128)(2,1)}, u32[]{:S(2)}) copy-start(bf16[384,1152]{1,0:T(8,128)(2,1)} %refs_4_.1) | copy-start | bytes 2654212
  33.7 13.5 %copy-start.2 = (bf16[384,384]{1,0:T(8,128)(2,1)S(1)}, bf16[384,384]{1,0:T(8,128)(2,1)}, u32[]{:S(2)}) copy-start(bf16[384,384]{1,0:T(8,128)(2,1)} %refs_6_.3) | copy-start | bytes 884740
  33.7 13.5 %copy-start.6 = (bf16[1,4,6,3,384]{4,1,3,2,0:T(4,128)(2,1)S(1)}, bf16[1,4,6,3,384]{4,1,3,2,0:T(4,128)(2,1)}, u32[]{:S(2)}) copy-start(bf16[1,4,6,3,384]{4,1,3,2,0:T(4,128)(2,1)} %param.37) | copy-start | bytes 165892
  33.7 13.5 %copy-start.7 = (f32[1152]{0:T(1024)S(1)}, f32[1152]{0:T(1024)}, u32[]{:S(2)}) copy-start(f32[1152]{0:T(1024)} %refs_5_.1) | copy-start | bytes 13828
  33.7 13.5 %copy-start.12 = (f32[384]{0:T(512)S(1)}, f32[384]{0:T(512)}, u32[]{:S(2)}) copy-start(f32[384]{0:T(512)} %refs_7_.3) | copy-start | bytes 4612

commit v5 on v4

--- a/solution.py
+++ b/solution.py
@@ -361,8 +361,9 @@
     return [pltpu.SemaphoreType.DMA((count,)) for count in counts for _ in range(2)]
 
 
-def halo_body(x_ref, low_ref, high_ref, tab_ref, tf_ref, tc_ref, *refs):
-    outs, biases, bufs, (ss, rs, ts, tr) = (refs[:5], refs[5:9], refs[9:15], refs[15:])
+def halo_body(cells_ref, tf_ref, tc_ref, x_out, *refs):
+    outs, biases, bufs = (refs[:5], refs[5:9], refs[9:15])
+    x_ref, low_ref, high_ref, tab_ref, stage, ss, rs, ts, tr = refs[15:]
     par, upo, upp, dno, dnp, tab = bufs
     lat, lon, up, down, partner = ring_positions()
     size = tab.shape[0]
@@ -370,7 +371,11 @@
     others = [lax.rem(rank + d, size) for d in range(1, size)]
     near = [(lat, lon - rank + other) for other in others]
     beside = (lat, partner)
-    meet([(up, lon), (down, lon), beside] + near)
+    peers = [(up, lon), (down, lon), beside] + near
+    greet(peers)
+    prepare_body(cells_ref, tf_ref, x_ref, low_ref, high_ref, tab_ref, stage)
+    x_out[...] = x_ref[...]
+    await_greetings(peers)
     low_copy = start_copy(low_ref, upo, ss.at[1], rs.at[1], (down, lon))
     high_copy = start_copy(high_ref, dno, ss.at[2], rs.at[2], (up, lon))
     table_copy = start_copy(tab_ref.at[rank], tab.at[rank], ss.at[3], rs.at[3], (up, lon))
@@ -1283,21 +1288,14 @@
     side = ((128, 128), BF16)
     own = ((FINE, C_F), BF16)
     table_part = ((group, PART_A // group, 128), BF16)
-    x, low, high, table_send = call(
-        prepare_body,
-        [own, side, side, table_part],
-        (cells, fine_rows),
-        [pltpu.VMEM((288, C_F), F32)],
-        "prepare",
-        2,
-    )
     halo = [own, side, side, side, side, table_part]
     bias_a, bias_b = (((2, 432, 144), F32), ((2, 240, 160), F32))
-    par, upo, upp, dno, dnp, bias_a, bias_b, bias_c, bias_q = remote_call(
+    x, par, upo, upp, dno, dnp, bias_a, bias_b, bias_c, bias_q = remote_call(
         halo_body,
-        halo[:5] + [bias_a, bias_b, bias_b, ((2, 432, 160), F32)],
-        (x, low, high, table_send, fine_rows, coarse_rows),
-        [pltpu.VMEM(*s) for s in halo] + semaphores(6, max(group - 1, 1)),
+        [own] + halo[:5] + [bias_a, bias_b, bias_b, ((2, 432, 160), F32)],
+        (cells, fine_rows, coarse_rows),
+        [pltpu.VMEM(*s) for s in halo + [own, side, side, table_part, ((288, C_F), F32)]]
+        + semaphores(6, max(group - 1, 1)),
         1,
         "halo",
         12,

time: 112 us -> 112 us (level)
    pallas_call x2 -> x1, Pallas kernels: 2.95 us -> 2.14 us  [call(): pl.pallas_call(body, out_shape=tuple((jax.ShapeDtypeStruct(shape, dtype)...]
where the time goes in v5:
time: 112 us; the launch traced here: 111 us
  Pallas kernels  102 us (91%)
  local copies, waits for them, and re-layouts  8.55 us (8%)
    pallas_call x4, Pallas kernels, remote_call(): pl.pallas_call(body, out_shape=tuple((jax.ShapeDtypeStruct(shape, dtype)...  99.8 us

profile of v5, /device:TPU:1, one launch (start us, length us, event | category | flops | bytes accessed | tf_op | source)
XLA Modules:
  0.0 111.4 jit_solution(693444094226957030)
XLA Ops:
  0.6 1.7 %reshape.28.tf_ref = bf16[576,138]{1,0:T(8,128)(2,1)S(1)} reshape(bf16[2,39744]{1,0:T(2,128)(2,1)} %param.26) | data formatting | bytes 317952 | tf_op jit(solution)/shard_map/reshape | solution.py:1282
  2.4 1.7 %reshape.29.tc_ref = bf16[576,138]{1,0:T(8,128)(2,1)S(1)} reshape(bf16[2,39744]{1,0:T(2,128)(2,1)} %param.36) | data formatting | bytes 317952 | tf_op jit(solution)/shard_map/reshape | solution.py:1283
  4.1 0.0 copy-start.4
  4.1 0.9 copy-done.4
  5.0 0.0 copy-start.9
  5.1 0.0 copy-start.10
  5.1 0.0 copy-start.11
  5.1 0.0 copy-start.13
  5.1 0.0 copy-start.14
  5.1 0.0 copy-start.15
  5.1 0.0 copy-start.16
  5.1 28.4 %halo.1 = (bf16[304,192]{1,0:T(8,128)(2,1)S(1)}, bf16[304,192]{1,0:T(8,128)(2,1)S(1)}, bf16[128,128]{1,0:T(8,128)(2,1)S(1)}, bf16[128,128]{1,0:T(8,128)(2,1)S(1)...) custom-call(bf16[12,6,4,192]{3,2,1,0:T(4,128)(2,1)S(1)} %bitcast.16,, ...), custom_call_target="tpu_custom_call" | custom-call | flops 24000000000 | bytes 44280000 | tf_op jit(solution)/shard_map/halo/pallas_call | solution.py:346
  33.5 0.0 copy-done.1
  33.5 0.0 copy-done.3
  33.6 0.0 copy-start
  33.6 0.0 copy-start.2
  33.6 0.0 copy-start.6
  33.6 0.0 copy-start.7
  33.7 0.0 copy-start.12
  33.7 13.4 %fine_forward_gather.1 = (f32[928,192]{1,0:T(8,128)S(1)}, bf16[928,192]{1,0:T(8,128)(2,1)S(1)}, f32[304,192]{1,0:T(8,128)S(1)}, f32[928,192]{1,0:T(8,128)S(1)}, ...) custom-call(bf16[304,192]{1,0:T(8,128)(2,1)S(1)} %get-tuple-element., ...), custom_call_target="tpu_custom_call" | custom-call | flops 22000001024 | bytes 40590000 | tf_op jit(solution)/shard_map/fine_forward_gather/pallas_call | solution.py:346
  47.1 0.0 copy-done
  47.1 0.0 copy-done.2
  47.1 0.0 copy-done.6
  47.1 0.0 copy-done.7
  47.2 0.0 copy-done.12
  47.2 13.4 %coarse_attention_scatter.1 = (bf16[6,3,4,384]{3,2,1,0:T(4,128)(2,1)S(1)}, f32[80,384]{1,0:T(8,128)S(1)}, f32[80,384]{1,0:T(8,128)S(1)}, f32[4620,128]{1,0:T(8,1...) custom-call(bf16[4,80,384]{2,1,0:T(8,128)(2,1)S(1)} %get-tuple-element.54.refs_0_, ...), custom_call_target="tpu_custom_call" | custom-call | flops 24000000000 | bytes 44280000 | tf_op jit(solution)/shard_map/coarse_attention_scatter/pallas_call | solution.py:346
  60.6 44.6 %fine_backward_reduce.1 = (f32[304,192]{1,0:T(8,128)S(1)}, f32[304,192]{1,0:T(8,128)S(1)}, f32[128,128]{1,0:T(8,128)S(1)}, bf16[2,4,8,32,128]{4,3,2,1,0:T(8,128)...) custom-call(f32[80,384]{1,0:T(8,128)S(1)} %get-tuple-element.59.refs_0_, ...), custom_call_target="tpu_custom_call" | custom-call | flops 80000000000 | bytes 147600000 | tf_op jit(solution)/shard_map/fine_backward_reduce/pallas_call | solution.py:346
  105.2 2.1 %final.1 = (bf16[12,6,4,192]{3,2,1,0:T(4,128)(2,1)}, f32[576,138]{1,0:T(8,128)S(1)}, f32[576,138]{1,0:T(8,128)S(1)}) custom-call(bf16[304,192]{1,0:T(8,128)(2,1)S(1)} %get-tuple-element.45.refs_0_.x_ref, f32[192]{0:T(256)S(1)} %copy-done.16, f32[304,192]{1,0:T(8,128)S(1)} %get-tuple-element.75.fog_ref, f32[304,192]{1,0:T(8,128)S(1)} %get-tuple-element.76.own_ref, ...), custom_call_target="tpu_custom_call" | custom-call | flops 4000000000 | bytes 7380000 | tf_op jit(solution)/shard_map/final/pallas_call | solution.py:256
  107.3 0.7 dynamic_slice.3
  108.0 1.4 %reshape.32 = f32[2,39744]{1,0:T(2,128)} reshape(f32[576,138]{1,0:T(8,128)S(1)} %get-tuple-element.83) | data formatting | bytes 635904 | tf_op jit(solution)/shard_map/reshape | solution.py:1458
  109.4 1.4 %reshape.33 = f32[2,39744]{1,0:T(2,128)} reshape(f32[576,138]{1,0:T(8,128)S(1)} %get-tuple-element.84) | data formatting | bytes 635904 | tf_op jit(solution)/shard_map/reshape | solution.py:1459
  110.8 0.6 copy.25
  (13 shorter events, 0.0 us)
Async XLA Ops:
  4.1 0.9 copy-start.4
  5.0 28.5 %copy-start.1 = (bf16[768,384]{1,0:T(8,128)(2,1)S(1)}, bf16[768,384]{1,0:T(8,128)(2,1)}, u32[]{:S(2)}) copy-start(bf16[768,384]{1,0:T(8,128)(2,1)} %refs_18_.1) | copy-start | bytes 1769476
  5.0 28.5 %copy-start.3 = (bf16[192,576]{1,0:T(8,128)(2,1)S(1)}, bf16[192,576]{1,0:T(8,128)(2,1)}, u32[]{:S(2)}) copy-start(bf16[192,576]{1,0:T(8,128)(2,1)} %refs_15_.3) | copy-start | bytes 663556
  5.0 28.5 %copy-start.5 = (bf16[192,192]{1,0:T(8,128)(2,1)S(1)}, bf16[192,192]{1,0:T(8,128)(2,1)}, u32[]{:S(2)}) copy-start(bf16[192,192]{1,0:T(8,128)(2,1)} %refs_19_.1) | copy-start | bytes 221188
  5.0 28.5 %copy-start.8 = (f32[576]{0:T(1024)S(1)}, f32[576]{0:T(1024)}, u32[]{:S(2)}) copy-start(f32[576]{0:T(1024)} %refs_9_.1) | copy-start | bytes 6916
  5.0 28.5 %copy-start.9 = (f32[768]{0:T(1024)S(1)}, f32[768]{0:T(1024)}, u32[]{:S(2)}) copy-start(f32[768]{0:T(1024)} %refs_13_.1) | copy-start | bytes 9220
  5.1 28.5 %copy-start.10 = (f32[768]{0:T(1024)S(1)}, f32[768]{0:T(1024)}, u32[]{:S(2)}) copy-start(f32[768]{0:T(1024)} %refs_17_.1) | copy-start | bytes 9220
  5.1 28.5 %copy-start.11 = (f32[384]{0:T(512)S(1)}, f32[384]{0:T(512)}, u32[]{:S(2)}) copy-start(f32[384]{0:T(512)} %refs_16_.2) | copy-start | bytes 4612
  5.1 28.5 %copy-start.13 = (f32[384]{0:T(512)S(1)}, f32[384]{0:T(512)}, u32[]{:S(2)}) copy-start(f32[384]{0:T(512)} %refs_16_.3) | copy-start | bytes 4612
  5.1 28.5 %copy-start.14 = (f32[192]{0:T(256)S(1)}, f32[192]{0:T(256)}, u32[]{:S(2)}) copy-start(f32[192]{0:T(256)} %refs_7_.2) | copy-start | bytes 2308
  5.1 28.5 %copy-start.15 = (f32[192]{0:T(256)S(1)}, f32[192]{0:T(256)}, u32[]{:S(2)}) copy-start(f32[192]{0:T(256)} %refs_11_.1) | copy-start | bytes 2308
  5.1 28.5 %copy-start.16 = (f32[192]{0:T(256)S(1)}, f32[192]{0:T(256)}, u32[]{:S(2)}) copy-start(f32[192]{0:T(256)} %gain_ref.1) | copy-start | bytes 2308
  33.6 13.5 %copy-start = (bf16[384,1152]{1,0:T(8,128)(2,1)S(1)}, bf16[384,1152]{1,0:T(8,128)(2,1)}, u32[]{:S(2)}) copy-start(bf16[384,1152]{1,0:T(8,128)(2,1)} %refs_4_.1) | copy-start | bytes 2654212
  33.6 13.5 %copy-start.2 = (bf16[384,384]{1,0:T(8,128)(2,1)S(1)}, bf16[384,384]{1,0:T(8,128)(2,1)}, u32[]{:S(2)}) copy-start(bf16[384,384]{1,0:T(8,128)(2,1)} %refs_6_.3) | copy-start | bytes 884740
  33.6 13.5 %copy-start.6 = (bf16[1,4,6,3,384]{4,1,3,2,0:T(4,128)(2,1)S(1)}, bf16[1,4,6,3,384]{4,1,3,2,0:T(4,128)(2,1)}, u32[]{:S(2)}) copy-start(bf16[1,4,6,3,384]{4,1,3,2,0:T(4,128)(2,1)} %param.37) | copy-start | bytes 165892
  33.6 13.5 %copy-start.7 = (f32[1152]{0:T(1024)S(1)}, f32[1152]{0:T(1024)}, u32[]{:S(2)}) copy-start(f32[1152]{0:T(1024)} %refs_5_.1) | copy-start | bytes 13828
  33.7 13.5 %copy-start.12 = (f32[384]{0:T(512)S(1)}, f32[384]{0:T(512)}, u32[]{:S(2)}) copy-start(f32[384]{0:T(512)} %refs_7_.3) | copy-start | bytes 4612
